TPU v7x, 128 devices: a whole 4x4x4 slice. The times are simulated.
128 devices in a mesh: acq: 8 (over y, z_hi), strip: 16 (over z_lo, x, core).
Axes of the slice: x: 4, y: 4, z: 4 (z_hi: 2, z_lo: 2; z = z_hi * 2 + z_lo), core: 2. Of those that a mesh axis runs over, the one named last changes fastest.
Arguments:
- raw_echo_values: float32 [16, 16, 8, 120, 2, 512], P('strip', None, None, 'acq')
- cell_target_line: int32 [16, 16, 8], P('strip'), may hold values from -1 to 63, as said below
- cell_track_displacement: int32 [16, 16, 8], P('strip'), may hold values from -48 to 48
- along_track_chirp_slope: float32 [120], P('acq'), may hold values from 0.001 to 0.01
- along_track_look_radius: int32 [128], P('strip'), may hold values from 5 to 7
- range_look_radius: int32 [64], replicated, may hold values from 3 to 7
Outputs:
- coherence: float32 [120, 120, 2, 8192], P('acq', None, None, 'strip')
Inputs may be any that keep to these rules, and one draw needn't show every extreme that they name: `cell_target_line`: in each reader's group of 8 slots for one strip the live slots come first; every row of every strip is named by at least one slot; some groups are full.
All inputs are finite; a program needn't handle non-finite values.
Results may differ from a plain program's by a relative error of at most 0.00065.
Values may be sent and summed in bfloat16 or wider, within the bound.
A program may use at most 320 MiB of HBM per device.

v0:
```python
import jax
import jax.numpy as jnp
from jax import lax
from jax.sharding import PartitionSpec as P

epsilon = 1e-06


def extended(value, sides, width):
    for axis, dim in sides:
        devices, length = (lax.axis_size(axis), value.shape[dim])
        up = [(i, (i + 1) % devices) for i in range(devices - 1)]
        down = [(j, i) for i, j in up]
        last = lax.slice_in_dim(value, length - width, length, axis=dim)
        initial = lax.slice_in_dim(value, 0, width, axis=dim)
        before = lax.ppermute(last, axis, up)
        after = lax.ppermute(initial, axis, down)
        value = jnp.concatenate([before, value, after], axis=dim)
    return value


def subtract_linear_chirp(raw_echo_values, cell_track_displacement, along_track_chirp_slope):
    squared = cell_track_displacement.astype(jnp.float32) ** 2
    phase = squared[..., None] * along_track_chirp_slope
    cosine = jnp.cos(phase)[..., None]
    sine_part = jnp.sin(phase)[..., None]
    inphase_source = raw_echo_values[..., 0, :]
    quadrature_source = raw_echo_values[..., 1, :]
    real_out = inphase_source * cosine + quadrature_source * sine_part
    imag_out = quadrature_source * cosine - inphase_source * sine_part
    return jnp.stack([real_out, imag_out], axis=-2)


def windows_of(padded):
    inner = padded.shape[2] - 8
    acq_count = padded.shape[0]
    columns = padded.shape[3]
    upper = padded[:, :, :inner].reshape(acq_count, 2, inner // 8, 8, columns)
    lower = padded[:, :, 8:].reshape(acq_count, 2, inner // 8, 8, columns)
    return jnp.concatenate([upper, lower], axis=3)


def look(values, colmask):
    return jnp.einsum("...c,cq->...q", values, colmask, precision=lax.Precision.HIGHEST)


def power_of(win, weight):
    weighted = win * weight[None, None, :, :, None]
    total = None
    for part_index in range(2):
        for offset_index in range(16):
            left_rows = weighted[:, part_index, :, offset_index, :].astype(jnp.float32)
            right_rows = win[:, part_index, :, offset_index, :].astype(jnp.float32)
            term = left_rows * right_rows
            total = term if total is None else total + term
    return total


def pair_sums(weighted, right_win):
    real_sum = None
    imag_sum = None
    for offset_index in range(16):
        left_real = weighted[:, 0, :, offset_index, :].astype(jnp.float32)[:, None]
        left_imag = weighted[:, 1, :, offset_index, :].astype(jnp.float32)[:, None]
        right_real = right_win[:, 0, :, offset_index, :].astype(jnp.float32)[None]
        right_imag = right_win[:, 1, :, offset_index, :].astype(jnp.float32)[None]
        real_term = left_real * right_real + left_imag * right_imag
        imag_term = left_imag * right_real - left_real * right_imag
        real_sum = real_term if real_sum is None else real_sum + real_term
        imag_sum = imag_term if imag_sum is None else imag_sum + imag_term
    return (real_sum, imag_sum)


def coherence_block(left_win, left_power, right_win, weight, colmask):
    weighted = left_win * weight[None, None, :, :, None]
    real_sum, imag_sum = pair_sums(weighted, right_win)
    right_power = look(power_of(right_win, weight), colmask)
    scale = 1.0 / jnp.sqrt(left_power[:, None] * right_power[None] + epsilon)
    real_look = look(real_sum, colmask) * scale
    imag_look = look(imag_sum, colmask) * scale
    stacked = jnp.stack([real_look, imag_look], axis=2)
    return stacked.reshape(stacked.shape[0], stacked.shape[1], 2, -1)


def per_device(
    raw_echo_values,
    cell_target_line,
    cell_track_displacement,
    along_track_chirp_slope,
    along_track_look_radius,
    range_look_radius,
):
    received, rows_in, offsets_in = (
        lax.all_to_all(raw_echo_values, "strip", split_axis=1, concat_axis=0, tiled=True),
        lax.all_to_all(cell_target_line, "strip", split_axis=1, concat_axis=0, tiled=True),
        lax.all_to_all(cell_track_displacement, "strip", split_axis=1, concat_axis=0, tiled=True),
    )
    levelled_echoes = subtract_linear_chirp(received, offsets_in, along_track_chirp_slope).astype(
        jnp.bfloat16
    )
    columns = levelled_echoes.shape[5]
    strip_rows = along_track_look_radius.shape[0] * 8
    out_cols = range_look_radius.shape[0]
    selector = rows_in[None] == jnp.arange(strip_rows, dtype=jnp.int32)[:, None, None, None]
    counts = jnp.sum(selector.astype(jnp.float32), axis=(1, 2, 3))
    onehot = selector.astype(jnp.bfloat16)
    summed = jnp.einsum(
        "xrdk,rdkapc->apxc", onehot, levelled_echoes, preferred_element_type=jnp.float32
    )
    tile = (summed / counts[None, None, :, None]).astype(jnp.bfloat16)
    padded = extended(tile, (("strip", 2),), 4)
    offsets_row = jnp.abs(jnp.arange(16, dtype=jnp.int32) - 8)
    weight = (offsets_row[None, :] <= along_track_look_radius[:, None]).astype(jnp.bfloat16)
    centres = 8 * jnp.arange(out_cols, dtype=jnp.int32) + 4
    distance = jnp.abs(jnp.arange(columns, dtype=jnp.int32)[:, None] - centres[None, :])
    colmask = (distance <= range_look_radius[None, :]).astype(jnp.float32)
    local_win = windows_of(padded)
    local_power = look(power_of(local_win, weight), colmask)
    return coherence_block(
        local_win,
        local_power,
        windows_of(lax.all_gather(padded, "acq", axis=0, tiled=True)),
        weight,
        colmask,
    )


def solution(mesh):
    placed = (
        P("strip", None, None, "acq", None, None),
        P("strip", None, None),
        P("strip", None, None),
        P("acq"),
        P("strip"),
        P(),
    )
    return jax.shard_map(
        per_device,
        mesh=mesh,
        in_specs=placed,
        out_specs=P("acq", None, None, "strip"),
        check_vma=False,
    )
```

profile of v0, /device:TPU:1, one launch (start us, length us, event | category | flops | bytes accessed | tf_op | source)
XLA Modules:
  0.0 846.5 jit_solution(6525421511408570551)
XLA Ops:
  7.9 7.2 all-to-all-start.1
  16.4 4.1 all-to-all-done.1
  20.5 3.9 all-to-all-start.2
  24.5 7.9 copy.233
  32.3 5.9 all-to-all-start
  38.9 104.9 %all-to-all-done = f32[1,16,8,15,2,512]{5,2,3,4,0,1:T(8,128)} async-done(((f32[1,16,8,15,2,512]{5,2,3,4,0,1:T(8,128)}), f32[1,16,8,15,2,512]{5,2,3,4,0,1:T(8,128)}, u32[]{:S(2)}, u32[]{:S(2)}) %all-to-all-start) | async-done | bytes 7864352 | tf_op jit(solution)/shard_map/all_to_all | solution.py:94
  143.7 10.3 %copy.317 = f32[1,16,8,15,2,512]{5,1,2,3,4,0:T(8,128)S(1)} copy(f32[1,16,8,15,2,512]{5,2,3,4,0,1:T(8,128)} %all-to-all-done) | data formatting | bytes 15728640 | tf_op jit(solution)/shard_map/all_to_all | solution.py:94
  156.5 4.8 collective-permute-start
  163.3 4.3 collective-permute-done.1
  167.5 2.6 pad_maximum_fusion.1
  179.6 186.8 %all-gather.2.cloned.1.call-done = bf16[120,2,72,512]{3,2,1,0:T(8,128)(2,1)} async-done(((bf16[15,2,72,512]{3,2,1,0:T(8,128)(2,1)}), bf16[120,2,72,512]{3,2,1,0:T(8,128)(2,1)}) %all-gather.2.cloned.1.call-update) | async-done | bytes 17694736 | tf_op jit(solution)/shard_map/all_gather | solution.py:122
  366.4 12.1 %slice_bitcast_fusion.1 = (bf16[120,2,8,8,512]{4,3,2,1,0:T(8,128)(2,1)S(1)}, bf16[120,2,8,8,512]{4,3,2,1,0:T(8,128)(2,1)S(1)}) fusion(bf16[120,2,72,512]{3,2,1,0:T(8,128)(2,1)} %all-gather.2.cloned.1.call-done), kind=kLoop, calls=%fused_computation.130 | loop fusion | bytes 62914560 | tf_op jit(solution)/shard_map/reshape | solution.py:38
  378.5 11.3 %copy.243 = bf16[120,2,8,8,512]{4,2,0,3,1:T(8,128)(2,1)} copy(bf16[120,2,8,8,512]{4,3,2,1,0:T(8,128)(2,1)S(1)} %get-tuple-element.5) | data formatting | bytes 31457280 | tf_op jit(solution)/shard_map/reshape | solution.py:38
  389.8 11.2 %copy.259 = bf16[120,2,8,8,512]{4,2,0,3,1:T(8,128)(2,1)} copy(bf16[120,2,8,8,512]{4,3,2,1,0:T(8,128)(2,1)S(1)} %get-tuple-element.6) | data formatting | bytes 31457280 | tf_op jit(solution)/shard_map/reshape | solution.py:39
  401.1 14.0 %fusion.370 = (f32[120,8,512]{2,1,0:T(8,128)S(1)}, f32[120,8,512]{2,1,0:T(8,128)}, f32[120,8,512]{2,1,0:T(8,128)}, f32[120,8,512]{2,1,0:T(8,128)}, f32[120,8,512...) fusion(bf16[120,2,8,8,512]{4,2,0,3,1:T(8,128)(2,1)} %copy.243), kind=kLoop, calls=%fused_computation.440 | loop fusion | flops 7864320 | bytes 47185920 | tf_op jit(solution)/shard_map/convert_element_type | solution.py:65
  415.1 21.4 %maximum_multiply_fusion = bf16[120,2,8,16,512]{4,2,0,3,1:T(8,128)(2,1)} fusion(bf16[120,2,8,8,512]{4,2,0,3,1:T(8,128)(2,1)} %copy.259, bf16[120,2,8,8,512]{4,2,0,3,1:T(8,128)(2,1)} %copy.243, bf16[8,16]{0,1:T(8,128)(2,1)S(1)} %compare_convert_fusion), kind=kLoop, calls=%fused_computation | loop fusion | flops 31457280 | bytes 62914816 | tf_op jit(solution)/shard_map/mul | solution.py:48
  436.5 14.5 %fusion.354 = (f32[120,8,512]{2,1,0:T(8,128)}, f32[120,8,512]{2,1,0:T(8,128)}, f32[120,8,512]{2,1,0:T(8,128)}, f32[120,8,512]{2,1,0:T(8,128)}, f32[120,8,512]{2,...) fusion(bf16[120,2,8,8,512]{4,2,0,3,1:T(8,128)(2,1)} %copy.259), kind=kLoop, calls=%fused_computation.408 | loop fusion | flops 7864320 | bytes 47185920 | tf_op jit(solution)/shard_map/convert_element_type | solution.py:65
  451.0 21.9 %fusion.274 = f32[120,8,64]{2,1,0:T(8,128)S(1)} fusion(bf16[120,2,8,16,512]{4,2,0,3,1:T(8,128)(2,1)} %maximum_multiply_fusion, bf16[120,2,8,8,512]{4,2,0,3,1:T(8,128)(2,1)} %copy.243, bf16[120,2,8,8,512]{4,2,0,3,1:T(8,128)(2,1)} %copy.259, s32[64]{0:T(128)S(1)} %copy-done.1, s32[64]{0:T(128)S(1)} %multiply_add_fusion), kind=kOutput, calls=%fused_computation.282 | convolution fusion | flops 440008704 | bytes 63160832 | tf_op jit(solution)/shard_map/...c,cq->...q/dot_general | solution.py:44
  472.9 177.8 %fusion.257 = f32[15,120,8,64]{3,2,1,0:T(8,128)} fusion(f32[120,8,64]{2,1,0:T(8,128)S(1)} %fusion.274, f32[15,8,64]{2,1,0:T(8,128)S(1)} %fusion.404, f32[120,8,512]{2,1,0:T(8,128)} %get-tuple-element.24, f32[15,8,512]{2,1,0:T(8,128)} %get-tuple-element.42, f32[120,8,512]{2,1,0:T(8,128)} %get-tuple-element.25, f32[15,8,512]{2,1,0:T(8,128)} %get-tuple-element.43, ...), kind=kOutput, calls=%fused_computation.263 | convolution fusion | flops 6129561600 | bytes 74774528 | tf_op jit(solution)/shard_map/...c,cq->...q/dot_general | solution.py:44
  650.7 6.4 copy.309
  657.2 157.5 %fusion.256 = f32[15,120,8,64]{3,2,1,0:T(8,128)} fusion(f32[120,8,64]{2,1,0:T(8,128)S(1)} %fusion.274, f32[15,8,64]{2,1,0:T(8,128)S(1)} %fusion.404, f32[120,8,512]{2,1,0:T(8,128)} %get-tuple-element.24, f32[15,8,512]{2,1,0:T(8,128)} %get-tuple-element.42, f32[120,8,512]{2,1,0:T(8,128)} %get-tuple-element.25, f32[15,8,512]{2,1,0:T(8,128)} %get-tuple-element.43, ...), kind=kOutput, calls=%fused_computation.262 | convolution fusion | flops 6129561600 | bytes 74774528 | tf_op jit(solution)/shard_map/...c,cq->...q/dot_general | solution.py:44
  814.6 6.5 copy.310
  821.1 7.2 pad_maximum_fusion
  828.3 10.9 %copy.311 = f32[15,120,2,512]{3,2,1,0:T(2,128)} copy(f32[15,120,2,512]{1,3,0,2:T(8,128)} %pad_maximum_fusion) | data formatting | bytes 14745600 | tf_op jit(solution)/shard_map/stack | solution.py:81
  (35 shorter events, 17.1 us)
Async XLA Ops:
  7.9 12.7 %all-to-all-start.1 = ((s32[1,16,8]{2,0,1:T(1,128)}), s32[1,16,8]{2,0,1:T(1,128)S(1)}, u32[]{:S(2)}, u32[]{:S(2)}) async-start(s32[1,16,8]{2,0,1:T(1,128)} %copy.235), calls=%async_computation.1 | async-start | bytes 16384 | tf_op jit(solution)/shard_map/all_to_all | solution.py:96
  20.5 11.8 %all-to-all-start.2 = ((s32[1,16,8]{2,0,1:T(1,128)}), s32[1,16,8]{2,0,1:T(1,128)S(1)}, u32[]{:S(2)}, u32[]{:S(2)}) async-start(s32[1,16,8]{2,0,1:T(1,128)} %copy.238), calls=%async_computation.2 | async-start | bytes 16384 | tf_op jit(solution)/shard_map/all_to_all | solution.py:95
  32.3 6.2 copy-start.2
  32.3 111.4 %all-to-all-start = ((f32[1,16,8,15,2,512]{5,2,3,4,0,1:T(8,128)}), f32[1,16,8,15,2,512]{5,2,3,4,0,1:T(8,128)}, u32[]{:S(2)}, u32[]{:S(2)}) async-start(f32[1,16,8,15,2,512]{5,2,3,4,0,1:T(8,128)} %copy.233), calls=%async_computation | async-start | bytes 15728640 | tf_op jit(solution)/shard_map/all_to_all | solution.py:94
  38.3 328.1 %all-gather.2.cloned.1.call-start = ((), (), s32[]{:S(2)}) async-start(), calls=%async_computation.3 | async-start | bytes 19906560 | tf_op jit(solution)/shard_map/all_gather | solution.py:122
  156.5 6.7 collective-permute-start
  161.3 6.2 collective-permute-start.1
  170.2 0.7 copy-start.3
  170.2 0.7 copy-start.1
  650.7 6.4 copy-start
Sparse Core Ops, SparseCore 0:
  170.3 196.0 all-gather.1
where the time goes:
time: 856 us; the launch traced here: 846 us
  matrix products  360 us (42%)
  waiting for transfers between devices  300 us (35%)
  local copies, waits for them, and re-layouts  81.5 us (10%)
  other arithmetic  67.4 us (8%)
  starting transfers between devices  23.8 us (3%)
  between operations  14 us (2%)
    dot_general x4, matrix products, look(): jnp.einsum('...c,cq->...q', values, colmask, precision=lax.Precision.HIGH...  358 us
    all_gather x1, waiting for transfers between devices, per_device(): lax.all_gather(padded, 'acq', axis=0, tiled=True)  187 us
    all_to_all x1, waiting for transfers between devices, per_device(): lax.all_to_all(raw_echo_values, 'strip', split_axis=1, concat_axis=0, til...  105 us
    convert_element_type x2, other arithmetic, pair_sums(): right_real = right_win[:, 0, :, offset_index, :].astype(jnp.float32)[None]  28.5 us
    reshape x3, local copies, waits for them, and re-layouts, windows_of(): upper = padded[:, :, :inner].reshape(acq_count, 2, inner // 8, 8, columns)  24.1 us
    mul x1, other arithmetic, power_of(): weighted = win * weight[None, None, :, :, None]  21.4 us
  transfers between devices with their start and end apart: 6, of which 4 were waited for; matrix products, arithmetic and copies ran while one was open for 2% of the time, Pallas kernels for 0%

commit v1 on v0

v1 whole, which is shorter than its diff:
```python
import jax
import jax.numpy as jnp
from jax import lax
from jax.experimental import pallas as pl
from jax.experimental.pallas import tpu as pltpu
from jax.sharding import PartitionSpec as P

epsilon = 1e-06
N_STRIP = 16
N_GROUP = 8
CAP = 8
ACQ_LOC = 15
PIECE = 2176
ROW_LANE = 2160
CODE = 120.0
VMEM = 56 * 1024 * 1024


def params(limit=VMEM):
    return pltpu.CompilerParams(vmem_limit_bytes=limit)


def pack_kernel(raw_ref, ramp_ref, out_ref):
    ramp = ramp_ref[0]
    lane = lax.broadcasted_iota(jnp.int32, (CAP, 128), 1)
    low = lane < 64
    zero = jnp.zeros((CAP, 128), jnp.float32)
    halo = [[zero, jnp.where(lane == ROW_LANE - 2048, ramp[:, 127:128], 0.0)] for _ in range(N_GROUP)]
    for acq in range(ACQ_LOC):
        cosine = jnp.broadcast_to(ramp[:, acq : acq + 1], (CAP, 128))
        sine = jnp.broadcast_to(ramp[:, 64 + acq : 65 + acq], (CAP, 128))
        tiles = [[], []]
        for t in range(4):
            row = acq * 8 + t * 2
            real = raw_ref[0, pl.ds(row, CAP, stride=ACQ_LOC * 8), :]
            imag = raw_ref[0, pl.ds(row + 1, CAP, stride=ACQ_LOC * 8), :]
            new_real = real * cosine + imag * sine
            new_imag = imag * cosine - real * sine
            tiles[0].append(new_real)
            tiles[1].append(new_imag)
            even = jnp.where(low, new_real, pltpu.roll(new_imag, 64, 1))
            odd = jnp.where(low, pltpu.roll(new_real, 64, 1), new_imag)
            out_ref[2 * t, 0, :, acq * 128 : acq * 128 + 128] = even.astype(jnp.bfloat16)
            out_ref[2 * t + 1, 0, :, acq * 128 : acq * 128 + 128] = odd.astype(jnp.bfloat16)
        for part in range(2):
            vreg = acq // 8
            base = (acq % 8) * 16 + part * 8
            left = (lane >= base) & (lane < base + 4)
            right = (lane >= base + 4) & (lane < base + 8)
            for bound in range(1, N_GROUP):
                t = bound // 2
                if bound % 2:
                    source, start = tiles[part][t], 60
                else:
                    source, start = jnp.where(low, tiles[part][t], tiles[part][t - 1]), 124
                moved = pltpu.roll(source, (base - start) % 128, 1)
                halo[bound][vreg] = jnp.where(left, moved, halo[bound][vreg])
                halo[bound - 1][vreg] = jnp.where(right, moved, halo[bound - 1][vreg])
    for group in range(N_GROUP):
        for vreg in range(2):
            at = ACQ_LOC * 128 + vreg * 128
            out_ref[group, 0, :, at : at + 128] = halo[group][vreg].astype(jnp.bfloat16)


def edge_kernel(slots_ref, out_ref):
    slots = slots_ref[0]
    line = slots[:, ROW_LANE : ROW_LANE + 1].astype(jnp.float32)
    index = lax.broadcasted_iota(jnp.int32, (128, 16), 1)
    wanted = jnp.where(index < 4, index, jnp.where(index < 8, index + 56, 1000)).astype(jnp.float32)
    pick = (line == wanted).astype(jnp.float32).astype(jnp.bfloat16)
    dims = (((0,), (0,)), ((), ()))
    total = lax.dot_general(pick, slots, dims, preferred_element_type=jnp.float32)
    count = lax.dot_general(pick, jnp.ones((128, 128), jnp.bfloat16), dims, preferred_element_type=jnp.float32)
    inverse = 1.0 / jnp.maximum(count[:, :1], 1.0)
    out_ref[0] = (total * inverse).astype(jnp.bfloat16)


def regroup_kernel(slots_ref, before_ref, after_ref, out_ref, lines_ref):
    slots = slots_ref[0]
    line = slots[:, ROW_LANE : ROW_LANE + 1].astype(jnp.float32)
    lane = lax.broadcasted_iota(jnp.int32, (128, 128), 1)
    row = 8 * (lane // 16) + lane % 16 - 4
    inside = (row >= 0) & (row < 64)
    pick = (line == jnp.where(inside, row, 1000).astype(jnp.float32)).astype(jnp.float32)
    lane16 = lax.broadcasted_iota(jnp.int32, (16, 128), 1)
    sub16 = lax.broadcasted_iota(jnp.int32, (16, 128), 0)
    pick_before = ((lane16 < 4) & (sub16 == lane16 + 4)).astype(jnp.float32)
    pick_after = ((lane16 >= 124) & (sub16 == lane16 - 124)).astype(jnp.float32)
    picks = jnp.concatenate([pick, pick_before, pick_after], axis=0)
    inverse = 1.0 / jnp.maximum(jnp.sum(picks, axis=0, keepdims=True), 1.0)
    rows = jnp.concatenate([slots, before_ref[0], after_ref[0]], axis=0)
    total = lax.dot_general(
        rows, picks.astype(jnp.bfloat16), (((0,), (0,)), ((), ())), preferred_element_type=jnp.float32
    )
    lines_ref[...] = total * inverse
    group = lane16 // 16
    for part in range(2):
        for block in range(9):
            v = []
            for c in range(8):
                col = 8 * block + c - 4
                if 0 <= col < 64:
                    at, step = part * 64 + col, 128
                else:
                    at, step = ACQ_LOC * 128 + part * 8 + c, 16
                v.append(lines_ref[pl.ds(at, 16, stride=step), :].astype(jnp.bfloat16))
            for bit in (1, 2, 4):
                clear = (group & bit) == 0
                for i in range(8):
                    if i & bit:
                        continue
                    a, b = v[i], v[i + bit]
                    v[i] = jnp.where(clear, a, pltpu.roll(b, 16 * bit, 1))
                    v[i + bit] = jnp.where(clear, pltpu.roll(a, 128 - 16 * bit, 1), b)
            for o in range(8):
                out_ref[o, part, block] = v[o]


def gram_kernel(win_ref, mask_ref, out_ref):
    row = lax.broadcasted_iota(jnp.int32, (128, 128), 0)
    col = lax.broadcasted_iota(jnp.int32, (128, 128), 1)
    diagonal = row == col
    spare = row % 16 == 15
    dims = (((1,), (1,)), ((), ()))
    for q in range(8):
        re = jnp.concatenate([win_ref[0, 0, q], win_ref[0, 0, q + 1]], axis=1)
        im = jnp.concatenate([win_ref[0, 1, q], win_ref[0, 1, q + 1]], axis=1)
        mask = jnp.concatenate([mask_ref[0, 2 * q : 2 * q + 1, :], mask_ref[0, 2 * q + 1 : 2 * q + 2, :]], axis=1)
        left = jnp.concatenate([re * mask, im * mask], axis=1)
        real = lax.dot_general(left, jnp.concatenate([re, im], axis=1), dims, preferred_element_type=jnp.float32)
        imag = lax.dot_general(left, jnp.concatenate([-im, re], axis=1), dims, preferred_element_type=jnp.float32)
        only = jnp.where(diagonal, real, 0.0)
        power_n = jnp.sum(only, axis=0, keepdims=True)
        power_m = jnp.sum(only, axis=1, keepdims=True)
        scale_n = jnp.where(power_n > 0, lax.rsqrt(power_n), 0.0) * CODE
        scale_m = jnp.where(power_m > 0, lax.rsqrt(power_m), 0.0)
        high = power_n.astype(jnp.bfloat16).astype(jnp.float32)
        code_real = jnp.where(spare, high, jnp.exp2(real * scale_m * scale_n))
        code_imag = jnp.where(spare, power_n - high, jnp.exp2(imag * scale_m * scale_n))
        out_ref[:, q, :, 0:128] = code_real.astype(jnp.bfloat16).reshape(8, 16, 128)
        out_ref[:, q, :, 128:256] = code_imag.astype(jnp.bfloat16).reshape(8, 16, 128)


def place_kernel(code_ref, out_ref, flat_ref, power_ref):
    m = pl.program_id(0)

    @pl.when(m == 0)
    def _():
        for o in range(8):
            for g in range(8):
                at = (o * 64 + g * 8) * 16
                block = code_ref[g, o * 8 : o * 8 + 8].astype(jnp.float32)
                block = block.reshape(128, 256)
                flat_ref[0, at : at + 128, :] = block[:, :128]
                flat_ref[1, at : at + 128, :] = block[:, 128:]
        high = flat_ref[0, pl.ds(15, 512, stride=16), :]
        rest = flat_ref[1, pl.ds(15, 512, stride=16), :]
        power_ref[...] = (high + rest).T

    power_n = power_ref[...]
    me = lax.axis_index("acq") * 16 + m
    power_m = power_ref[pl.ds(me, 1), :]
    scale = jnp.sqrt(power_n) * jnp.sqrt(power_m) * lax.rsqrt(power_n * power_m + epsilon)
    for part in range(2):
        codes = flat_ref[part, pl.ds(m, 512, stride=16), :].T
        scaled = jnp.log2(codes) * (1.0 / CODE) * scale
        for block in range(8):
            for t in range(4):
                piece = scaled[block * 16 : block * 16 + ACQ_LOC, t * 128 : t * 128 + 128]
                out_ref[0, pl.ds(block * ACQ_LOC * 8 + t * 2 + part, ACQ_LOC, stride=8), :] = piece


def per_device(
    raw_echo_values,
    cell_target_line,
    cell_track_displacement,
    along_track_chirp_slope,
    along_track_look_radius,
    range_look_radius,
):
    f32, bf16 = jnp.float32, jnp.bfloat16
    squared = cell_track_displacement[0].astype(f32) ** 2
    phase = squared[..., None] * along_track_chirp_slope
    line = cell_target_line[0].astype(f32)[..., None]
    gap = jnp.zeros((N_STRIP, CAP, 64 - ACQ_LOC), f32)
    ramp = jnp.concatenate([jnp.cos(phase), gap, jnp.sin(phase), gap[..., 1:], line], axis=-1)
    raw = raw_echo_values.reshape(N_STRIP, CAP, ACQ_LOC, 2, 4, 128)
    raw = raw.transpose(0, 1, 2, 4, 3, 5).reshape(N_STRIP, CAP * ACQ_LOC * 8, 128)
    packed = pl.pallas_call(
        pack_kernel,
        grid=(N_STRIP,),
        out_shape=jax.ShapeDtypeStruct((N_GROUP, N_STRIP, CAP, PIECE), bf16),
        in_specs=[
            pl.BlockSpec((1, CAP * ACQ_LOC * 8, 128), lambda s: (s, 0, 0)),
            pl.BlockSpec((1, CAP, 128), lambda s: (s, 0, 0)),
        ],
        out_specs=pl.BlockSpec((N_GROUP, 1, CAP, PIECE), lambda s: (0, s, 0, 0)),
        compiler_params=params(),
        name="pack",
    )(raw, ramp)
    packed = packed.reshape(N_GROUP * N_STRIP, CAP, PIECE)
    slots = lax.all_to_all(packed, ("acq", "strip"), split_axis=0, concat_axis=0, tiled=True)
    slots = slots.reshape(N_GROUP, N_STRIP * CAP, PIECE)
    edges = pl.pallas_call(
        edge_kernel,
        grid=(N_GROUP,),
        out_shape=jax.ShapeDtypeStruct((N_GROUP, 16, PIECE), bf16),
        in_specs=[pl.BlockSpec((1, 128, PIECE), lambda a: (a, 0, 0))],
        out_specs=pl.BlockSpec((1, 16, PIECE), lambda a: (a, 0, 0)),
        compiler_params=params(),
        name="edge",
    )(slots)
    count = lax.axis_size("strip")
    up = [(i, i + 1) for i in range(count - 1)]
    before = lax.ppermute(edges, "strip", up)
    after = lax.ppermute(edges, "strip", [(j, i) for i, j in up])
    windows = pl.pallas_call(
        regroup_kernel,
        grid=(N_GROUP,),
        out_shape=jax.ShapeDtypeStruct((8, 2, 9, 128, 128), bf16),
        in_specs=[
            pl.BlockSpec((1, 128, PIECE), lambda a: (a, 0, 0)),
            pl.BlockSpec((1, 16, PIECE), lambda a: (a, 0, 0)),
            pl.BlockSpec((1, 16, PIECE), lambda a: (a, 0, 0)),
        ],
        out_specs=pl.BlockSpec((8, 2, 9, 16, 128), lambda a: (0, 0, 0, a, 0)),
        scratch_shapes=[pltpu.VMEM((PIECE, 128), f32)],
        compiler_params=params(),
        name="regroup",
    )(slots, before, after)
    group = lax.axis_index("acq")
    radius = lax.dynamic_slice_in_dim(range_look_radius, group * 8, 8, 0)
    across = jnp.arange(16, dtype=jnp.int32)[None, :] - 8
    col_mask = (jnp.abs(across) <= radius[:, None]).reshape(8, 2, 8)
    row_mask = jnp.abs(across) <= along_track_look_radius[:, None]
    masks = (row_mask[:, None, None, None, :] & col_mask[None, :, :, :, None]).reshape(8, 16, 128).astype(bf16)
    codes = pl.pallas_call(
        gram_kernel,
        grid=(8,),
        out_shape=jax.ShapeDtypeStruct((8, 64, 16, 256), bf16),
        in_specs=[
            pl.BlockSpec((1, 2, 9, 128, 128), lambda o: (o, 0, 0, 0, 0)),
            pl.BlockSpec((1, 16, 128), lambda o: (o, 0, 0)),
        ],
        out_specs=pl.BlockSpec((8, 8, 16, 256), lambda o: (0, o, 0, 0)),
        compiler_params=params(),
        name="gram",
    )(windows, masks)
    received = lax.all_to_all(codes, "acq", split_axis=0, concat_axis=0, tiled=True)
    placed = pl.pallas_call(
        place_kernel,
        grid=(ACQ_LOC,),
        out_shape=jax.ShapeDtypeStruct((ACQ_LOC, 960, 128), f32),
        in_specs=[pl.BlockSpec((8, 64, 16, 256), lambda m: (0, 0, 0, 0))],
        out_specs=pl.BlockSpec((1, 960, 128), lambda m: (m, 0, 0)),
        scratch_shapes=[pltpu.VMEM((2, 512 * 16, 128), f32), pltpu.VMEM((128, 512), f32)],
        compiler_params=params(),
        name="place",
    )(received)
    placed = placed.reshape(ACQ_LOC, 120, 4, 2, 128).transpose(0, 1, 3, 2, 4)
    return placed.reshape(ACQ_LOC, 120, 2, 512)


def solution(mesh):
    placed = (
        P("strip", None, None, "acq", None, None),
        P("strip", None, None),
        P("strip", None, None),
        P("acq"),
        P("strip"),
        P(),
    )
    return jax.shard_map(
        per_device,
        mesh=mesh,
        in_specs=placed,
        out_specs=P("acq", None, None, "strip"),
        check_vma=False,
    )
```

time: 856 us -> 204 us (0.24)
  the two profiles are of different devices: /device:TPU:1 before, /device:TPU:7 now
where the time goes in v1:
time: 204 us; the launch traced here: 203 us
  Pallas kernels  64.6 us (32%)
  waiting for transfers between devices  59.7 us (29%)
  blocking collectives  54.7 us (27%)
  starting transfers between devices  18.8 us (9%)
  other arithmetic  3.14 us (2%)
  local copies, waits for them, and re-layouts  2.17 us (1%)
    all_to_all x1, blocking collectives, per_device(): lax.all_to_all(codes, 'acq', split_axis=0, concat_axis=0, tiled=True)  54.7 us
    all_to_all x1, waiting for transfers between devices, per_device(): lax.all_to_all(packed, ('acq', 'strip'), split_axis=0, concat_axis=0, til...  53.9 us
    pallas_call x1, Pallas kernels, per_device(): pl.pallas_call(pack_kernel, grid=(N_STRIP,), out_shape=jax.ShapeDtypeStru...  18.7 us
    pallas_call x1, Pallas kernels, per_device(): pl.pallas_call(regroup_kernel, grid=(N_GROUP,), out_shape=jax.ShapeDtypeS...  16.2 us
    pallas_call x1, Pallas kernels, per_device(): pl.pallas_call(place_kernel, grid=(ACQ_LOC,), out_shape=jax.ShapeDtypeStr...  12.6 us
    all_to_all x1, starting transfers between devices, per_device(): lax.all_to_all(packed, ('acq', 'strip'), split_axis=0, concat_axis=0, til...  11.2 us
    pallas_call x1, Pallas kernels, per_device(): pl.pallas_call(gram_kernel, grid=(8,), out_shape=jax.ShapeDtypeStruct((8,...  9.87 us
    pallas_call x1, Pallas kernels, per_device(): pl.pallas_call(edge_kernel, grid=(N_GROUP,), out_shape=jax.ShapeDtypeStru...  7.23 us
  transfers between devices with their start and end apart: 3, of which 3 were waited for; matrix products, arithmetic and copies ran while one was open for 1% of the time, Pallas kernels for 0%

profile of v1, /device:TPU:7, one launch (start us, length us, event | category | flops | bytes accessed | tf_op | source)
XLA Modules:
  0.0 203.3 jit_solution(9576137211227085773)
XLA Ops:
  0.0 0.7 convert_bitcast_fusion
  0.7 0.7 multiply_bitcast_fusion
  1.5 0.1 copy.9
  1.6 1.0 multiply_sine_fusion
  2.6 0.8 concatenate.3.ramp_ref
  3.3 18.7 %pack.1 = bf16[8,16,8,2176]{3,2,1,0:T(8,128)(2,1)} custom-call(f32[16,960,128]{2,1,0:T(8,128)} %bitcast.19, f32[16,8,128]{2,1,0:T(8,128)} %concatenate.3.ramp_ref), custom_call_target="tpu_custom_call" | custom-call | tf_op jit(solution)/shard_map/pack/pallas_call | solution.py:189
  22.1 11.2 %all-to-all-start = ((bf16[128,8,2176]{2,1,0:T(8,128)(2,1)}), bf16[128,8,2176]{2,1,0:T(8,128)(2,1)}, u32[]{:S(2)}, u32[]{:S(2)}) async-start(bf16[128,8,2176]{2,1,0:T(8,128)(2,1)} %bitcast.18), calls=%async_computation | async-start | bytes 8912896 | tf_op jit(solution)/shard_map/all_to_all | solution.py:202
  33.4 0.1 and.24
  33.5 0.1 dynamic_slice.3
  33.6 53.9 %all-to-all-done = bf16[128,8,2176]{2,1,0:T(8,128)(2,1)} async-done(((bf16[128,8,2176]{2,1,0:T(8,128)(2,1)}), bf16[128,8,2176]{2,1,0:T(8,128)(2,1)}, u32[]{:S(2)}, u32[]{:S(2)}) %all-to-all-start) | async-done | bytes 4456480 | tf_op jit(solution)/shard_map/all_to_all | solution.py:202
  87.4 7.2 %edge.1 = bf16[8,16,2176]{2,1,0:T(8,128)(2,1)} custom-call(bf16[8,128,2176]{2,1,0:T(8,128)(2,1)} %bitcast.6.slots_ref), custom_call_target="tpu_custom_call" | custom-call | tf_op jit(solution)/shard_map/edge/pallas_call | solution.py:204
  94.7 2.6 %collective-permute-start.1 = (bf16[8,16,2176]{2,1,0:T(8,128)(2,1)}, bf16[8,16,2176]{2,1,0:T(8,128)(2,1)S(1)}, u32[]{:S(2)}, u32[]{:S(2)}) collective-permute-start(bf16[8,16,2176]{2,1,0:T(8,128)(2,1)} %edge.1), channel_id=1, source_target_pairs={{1,0},{2,1},{3,2},{4,3},{5,4},{6,5},{7,6},{8,7},{9,8},{10,9},{11,1... | collective-permute-start | bytes 1671176 | tf_op jit(solution)/shard_map/ppermute | solution.py:216
  97.3 5.0 %collective-permute-start = (bf16[8,16,2176]{2,1,0:T(8,128)(2,1)}, bf16[8,16,2176]{2,1,0:T(8,128)(2,1)S(1)}, u32[]{:S(2)}, u32[]{:S(2)}) collective-permute-start(bf16[8,16,2176]{2,1,0:T(8,128)(2,1)} %edge.1), channel_id=1, source_target_pairs={{0,1},{1,2},{2,3},{3,4},{4,5},{5,6},{6,7},{7,8},{8,9},{9,10},{10,1... | collective-permute-start | bytes 1671176 | tf_op jit(solution)/shard_map/ppermute | solution.py:215
  102.4 0.1 broadcast_compare_fusion
  102.4 0.1 and.26
  102.5 0.1 and.27
  102.6 0.6 and_convert_fusion.mask_ref
  103.3 4.6 %collective-permute-done.1.after_ref = bf16[8,16,2176]{2,1,0:T(8,128)(2,1)S(1)} collective-permute-done((bf16[8,16,2176]{2,1,0:T(8,128)(2,1)}, bf16[8,16,2176]{2,1,0:T(8,128)(2,1)S(1)}, u32[]{:S(2)}, u32[]{:S(2)}) %collective-permute-start.1) | collective-permute-done | bytes 557088 | tf_op jit(solution)/shard_map/ppermute | solution.py:216
  107.8 1.3 collective-permute-done.before_ref
  109.1 0.8 copy-done.1
  109.9 16.2 %regroup.1.win_ref = bf16[8,2,9,128,128]{4,3,2,1,0:T(8,128)(2,1)} custom-call(bf16[8,128,2176]{2,1,0:T(8,128)(2,1)} %bitcast.6.slots_ref, bf16[8,16,2176]{2,1,0:T(8,128)(2,1)} %copy-done.1, bf16[8,16,2176]{2,1,0:T(8,128)(2,1)} %copy-done), custom_call_target="tpu_custom_call" | custom-call | tf_op jit(solution)/shard_map/regroup/pallas_call | solution.py:217
  126.1 9.9 %gram.1 = bf16[8,64,16,256]{3,2,1,0:T(8,128)(2,1)} custom-call(bf16[8,2,9,128,128]{4,3,2,1,0:T(8,128)(2,1)} %regroup.1.win_ref, bf16[8,16,128]{2,1,0:T(8,128)(2,1)} %and_convert_fusion.mask_ref), custom_call_target="tpu_custom_call" | custom-call | tf_op jit(solution)/shard_map/gram/pallas_call | solution.py:237
  136.0 54.7 %all_to_all.10.code_ref = bf16[8,64,16,256]{3,2,1,0:T(8,128)(2,1)} all-to-all(bf16[8,64,16,256]{3,2,1,0:T(8,128)(2,1)} %gram.1), channel_id=1, replica_groups=mesh['acq'=8,'strip'=16] {'acq'}, dimensions={0} | all-to-all | bytes 8388608 | tf_op jit(solution)/shard_map/all_to_all | solution.py:249
  190.7 12.6 %place.1 = f32[15,960,128]{2,1,0:T(8,128)} custom-call(bf16[8,64,16,256]{3,2,1,0:T(8,128)(2,1)} %all_to_all.10.code_ref), custom_call_target="tpu_custom_call" | custom-call | tf_op jit(solution)/shard_map/place/pallas_call | solution.py:250
  (14 shorter events, 0.2 us)
Async XLA Ops:
  22.1 11.2 %copy-start.2 = (s32[8]{0:T(128)S(1)}, s32[8]{0:T(128)}, u32[]{:S(2)}) copy-start(s32[8]{0:T(128)} %param.10) | copy-start | bytes 100
  22.1 11.4 %copy-start.3 = (s32[64]{0:T(128)S(1)}, s32[64]{0:T(128)}, u32[]{:S(2)}) copy-start(s32[64]{0:T(128)} %param.11) | copy-start | bytes 772
  22.1 65.4 %all-to-all-start = ((bf16[128,8,2176]{2,1,0:T(8,128)(2,1)}), bf16[128,8,2176]{2,1,0:T(8,128)(2,1)}, u32[]{:S(2)}, u32[]{:S(2)}) async-start(bf16[128,8,2176]{2,1,0:T(8,128)(2,1)} %bitcast.18), calls=%async_computation | async-start | bytes 8912896 | tf_op jit(solution)/shard_map/all_to_all | solution.py:202
  94.7 13.2 %collective-permute-start.1 = (bf16[8,16,2176]{2,1,0:T(8,128)(2,1)}, bf16[8,16,2176]{2,1,0:T(8,128)(2,1)S(1)}, u32[]{:S(2)}, u32[]{:S(2)}) collective-permute-start(bf16[8,16,2176]{2,1,0:T(8,128)(2,1)} %edge.1), channel_id=1, source_target_pairs={{1,0},{2,1},{3,2},{4,3},{5,4},{6,5},{7,6},{8,7},{9,8},{10,9},{11,1... | collective-permute-start | bytes 1671176 | tf_op jit(solution)/shard_map/ppermute | solution.py:216
  97.3 11.8 %collective-permute-start = (bf16[8,16,2176]{2,1,0:T(8,128)(2,1)}, bf16[8,16,2176]{2,1,0:T(8,128)(2,1)S(1)}, u32[]{:S(2)}, u32[]{:S(2)}) collective-permute-start(bf16[8,16,2176]{2,1,0:T(8,128)(2,1)} %edge.1), channel_id=1, source_target_pairs={{0,1},{1,2},{2,3},{3,4},{4,5},{5,6},{6,7},{7,8},{8,9},{9,10},{10,1... | collective-permute-start | bytes 1671176 | tf_op jit(solution)/shard_map/ppermute | solution.py:215
  107.8 1.3 copy-start
  109.1 0.8 copy-start.1

commit v2 on v1

v2 whole, which is shorter than its diff:
```python
import jax
import jax.numpy as jnp
from jax import lax
from jax.experimental import pallas as pl
from jax.experimental.pallas import tpu as pltpu
from jax.sharding import PartitionSpec as P

epsilon = 1e-06
N_STRIP = 16
N_GROUP = 8
CAP = 8
ACQ_LOC = 15
PIECE = 2176
ROW_LANE = 2160
CODE = 120.0
VMEM = 56 * 1024 * 1024


def params(limit=VMEM):
    return pltpu.CompilerParams(vmem_limit_bytes=limit)


def shift(place, strip_step, acq_step):
    acq, strip = place
    dx, dz, dc = (strip_step // 2) % 4, strip_step // 8, strip_step % 2
    dy, dh = acq_step // 2, acq_step % 2
    to_strip = ((strip // 8 + dz) % 2) * 8 + (((strip // 2) % 4 + dx) % 4) * 2 + (strip % 2 + dc) % 2
    to_acq = ((acq // 2 + dy) % 4) * 2 + (acq % 2 + dh) % 2
    return to_acq, to_strip


def strip_step(i):
    return (i * 11) % N_STRIP


def back(step):
    return (step // 8) * 8 + ((4 - (step // 2) % 4) % 4) * 2 + step % 2


def acq_step(n):
    half, rest = n // 4, n % 4
    dy = (1 - half) * (rest // 2) * 2 + half * (1 + 2 * (rest % 2))
    dh = (1 - half) * (rest % 2) + half * (rest // 2)
    return dy * 2 + dh


def acq_back(step):
    return ((4 - step // 2) % 4) * 2 + step % 2


def pack_tile(raw_ref, ramp_ref, packed_ref, s, t):
    ramp = ramp_ref[s]
    lane = lax.broadcasted_iota(jnp.int32, (CAP, 128), 1)
    low = lane < 64
    left_tile, right_tile = (t + 3) % 4, (t + 1) % 4
    kept = jnp.where(low, jnp.where(t < 3, 1.0, 0.0), jnp.where(t > 0, 1.0, 0.0))
    zero = jnp.zeros((CAP, 128), jnp.float32)
    line = jnp.where(lane == ROW_LANE - 2048, ramp[:, 127:128], 0.0)
    halo = [[zero, line], [zero, line]]

    def load(a, tile, part):
        return raw_ref[s, pl.ds(a * 8 + tile * 2 + part, CAP, stride=ACQ_LOC * 8), :]

    for a in range(ACQ_LOC):
        cosine = jnp.broadcast_to(ramp[:, a : a + 1], (CAP, 128))
        sine = jnp.broadcast_to(ramp[:, 64 + a : 65 + a], (CAP, 128))
        real, imag = load(a, t, 0), load(a, t, 1)
        main = [real * cosine + imag * sine, imag * cosine - real * sine]
        real = jnp.where(low, load(a, right_tile, 0), load(a, left_tile, 0)) * kept
        imag = jnp.where(low, load(a, right_tile, 1), load(a, left_tile, 1)) * kept
        outer = [real * cosine + imag * sine, imag * cosine - real * sine]
        even = jnp.where(low, main[0], pltpu.roll(main[1], 64, 1))
        odd = jnp.where(low, pltpu.roll(main[0], 64, 1), main[1])
        packed_ref[2 * t, s, :, a * 128 : a * 128 + 128] = even.astype(jnp.bfloat16)
        packed_ref[2 * t + 1, s, :, a * 128 : a * 128 + 128] = odd.astype(jnp.bfloat16)
        vreg = a // 8
        for part in range(2):
            base = (a % 8) * 16 + part * 8
            left = (lane >= base) & (lane < base + 4)
            right = (lane >= base + 4) & (lane < base + 8)
            inner = pltpu.roll(main[part], (base - 60) % 128, 1)
            edge = pltpu.roll(outer[part], (base - 124) % 128, 1)
            halo[0][vreg] = jnp.where(left, edge, jnp.where(right, inner, halo[0][vreg]))
            halo[1][vreg] = jnp.where(left, inner, jnp.where(right, edge, halo[1][vreg]))
    for side in range(2):
        for vreg in range(2):
            at = ACQ_LOC * 128 + vreg * 128
            packed_ref[2 * t + side, s, :, at : at + 128] = halo[side][vreg].astype(jnp.bfloat16)


def edge_rows(slots):
    line = slots[:, ROW_LANE : ROW_LANE + 1].astype(jnp.float32)
    index = lax.broadcasted_iota(jnp.int32, (128, 16), 1)
    wanted = jnp.where(index < 4, index, jnp.where(index < 8, index + 56, 1000)).astype(jnp.float32)
    pick = (line == wanted).astype(jnp.float32).astype(jnp.bfloat16)
    dims = (((0,), (0,)), ((), ()))
    total = lax.dot_general(pick, slots, dims, preferred_element_type=jnp.float32)
    count = lax.dot_general(pick, jnp.ones((128, 128), jnp.bfloat16), dims, preferred_element_type=jnp.float32)
    inverse = 1.0 / jnp.maximum(count[:, :1], 1.0)
    return (total * inverse).astype(jnp.bfloat16)


def regroup(slots, before, after, has_before, has_after, lines_ref, store):
    line = slots[:, ROW_LANE : ROW_LANE + 1].astype(jnp.float32)
    lane = lax.broadcasted_iota(jnp.int32, (128, 128), 1)
    row = 8 * (lane // 16) + lane % 16 - 4
    inside = (row >= 0) & (row < 64)
    pick = (line == jnp.where(inside, row, 1000).astype(jnp.float32)).astype(jnp.float32)
    lane16 = lax.broadcasted_iota(jnp.int32, (16, 128), 1)
    sub16 = lax.broadcasted_iota(jnp.int32, (16, 128), 0)
    pick_before = ((lane16 < 4) & (sub16 == lane16 + 4)).astype(jnp.float32) * has_before
    pick_after = ((lane16 >= 124) & (sub16 == lane16 - 124)).astype(jnp.float32) * has_after
    picks = jnp.concatenate([pick, pick_before, pick_after], axis=0)
    inverse = 1.0 / jnp.maximum(jnp.sum(picks, axis=0, keepdims=True), 1.0)
    rows = jnp.concatenate([slots, before, after], axis=0)
    total = lax.dot_general(
        rows, picks.astype(jnp.bfloat16), (((0,), (0,)), ((), ())), preferred_element_type=jnp.float32
    )
    lines_ref[...] = total * inverse
    group = lane16 // 16
    for part in range(2):
        for block in range(9):
            v = []
            for c in range(8):
                col = 8 * block + c - 4
                if 0 <= col < 64:
                    at, step = part * 64 + col, 128
                else:
                    at, step = ACQ_LOC * 128 + part * 8 + c, 16
                v.append(lines_ref[pl.ds(at, 16, stride=step), :].astype(jnp.bfloat16))
            for bit in (1, 2, 4):
                clear = (group & bit) == 0
                for i in range(8):
                    if i & bit:
                        continue
                    a, b = v[i], v[i + bit]
                    v[i] = jnp.where(clear, a, pltpu.roll(b, 16 * bit, 1))
                    v[i + bit] = jnp.where(clear, pltpu.roll(a, 128 - 16 * bit, 1), b)
            for o in range(8):
                store(o, part, block, v[o])


def gram(win_ref, mask_ref, o, store):
    row = lax.broadcasted_iota(jnp.int32, (128, 128), 0)
    col = lax.broadcasted_iota(jnp.int32, (128, 128), 1)
    diagonal = row == col
    spare = row % 16 == 15
    dims = (((1,), (1,)), ((), ()))
    for q in range(8):
        re = jnp.concatenate([win_ref[o, 0, q], win_ref[o, 0, q + 1]], axis=1)
        im = jnp.concatenate([win_ref[o, 1, q], win_ref[o, 1, q + 1]], axis=1)
        mask = jnp.concatenate([mask_ref[o, 2 * q : 2 * q + 1, :], mask_ref[o, 2 * q + 1 : 2 * q + 2, :]], axis=1)
        left = jnp.concatenate([re * mask, im * mask], axis=1)
        real = lax.dot_general(left, jnp.concatenate([re, im], axis=1), dims, preferred_element_type=jnp.float32)
        imag = lax.dot_general(left, jnp.concatenate([-im, re], axis=1), dims, preferred_element_type=jnp.float32)
        only = jnp.where(diagonal, real, 0.0)
        power_n = jnp.sum(only, axis=0, keepdims=True)
        power_m = jnp.sum(only, axis=1, keepdims=True)
        scale_n = jnp.where(power_n > 0, lax.rsqrt(power_n), 0.0) * CODE
        scale_m = jnp.where(power_m > 0, lax.rsqrt(power_m), 0.0)
        high = power_n.astype(jnp.bfloat16).astype(jnp.float32)
        code_real = jnp.where(spare, high, jnp.exp2(real * scale_m * scale_n))
        code_imag = jnp.where(spare, power_n - high, jnp.exp2(imag * scale_m * scale_n))
        store(q, code_real.astype(jnp.bfloat16).reshape(8, 16, 128), code_imag.astype(jnp.bfloat16).reshape(8, 16, 128))


def stack_kernel(
    raw_hbm, ramp_ref, mask_ref, out_ref,
    raw_ref, packed_ref, slots_ref, rows_ref, edges_ref, before_ref, after_ref, lines_ref, win_ref, code_ref,
    raw_sem, send_sem, recv_sem, own_sem, edge_send, edge_recv, code_send, code_recv, code_own,
):
    acq, strip = lax.axis_index("acq"), lax.axis_index("strip")
    place = (acq, strip)
    mesh_id = pl.DeviceIdType.MESH

    def device(to):
        return {"acq": to[0], "strip": to[1]}

    barrier = pltpu.get_barrier_semaphore()

    def greet(i, carry):
        pl.semaphore_signal(
            barrier, inc=1, device_id=device(shift(place, i % N_STRIP, i // N_STRIP)), device_id_type=mesh_id
        )
        return carry

    lax.fori_loop(1, N_STRIP * N_GROUP, greet, 0)

    def fetch(s):
        return pltpu.make_async_copy(raw_hbm.at[s], raw_ref.at[s], raw_sem.at[s])

    def fetch_start(i, carry):
        fetch(shift(place, strip_step(i), 0)[1]).start()
        return carry

    lax.fori_loop(0, N_STRIP, fetch_start, 0)
    pl.semaphore_wait(barrier, N_STRIP * N_GROUP - 1)

    own = pltpu.make_async_copy(packed_ref.at[acq, strip], slots_ref.at[acq, strip], own_sem)

    def slot_copy(n, i):
        to = shift(place, strip_step(i), acq_step(n))
        return pltpu.make_async_remote_copy(
            src_ref=packed_ref.at[to[0], to[1]],
            dst_ref=slots_ref.at[acq, strip],
            send_sem=send_sem.at[n * N_STRIP + i],
            recv_sem=recv_sem.at[n * N_STRIP + i],
            device_id=device(to),
            device_id_type=mesh_id,
        )

    def send(n, i):
        @pl.when(n * N_STRIP + i > 0)
        def _():
            slot_copy(n, i).start()

    y = acq // 2

    def early(i, carry):
        s = shift(place, strip_step(i), 0)[1]
        fetch(s).wait()
        pack_tile(raw_ref, ramp_ref, packed_ref, s, y)
        pack_tile(raw_ref, ramp_ref, packed_ref, s, (y + 2) % 4)

        @pl.when(i == 0)
        def _():
            own.start()

        for n in range(4):
            send(n, i)
        return carry

    lax.fori_loop(0, N_STRIP, early, 0)

    def late(i, carry):
        s = shift(place, strip_step(i), 0)[1]
        pack_tile(raw_ref, ramp_ref, packed_ref, s, (y + 1) % 4)
        pack_tile(raw_ref, ramp_ref, packed_ref, s, (y + 3) % 4)
        return carry

    lax.fori_loop(0, N_STRIP, late, 0)

    def late_send(j, carry):
        send(4 + j // N_STRIP, j % N_STRIP)
        return carry

    lax.fori_loop(0, 4 * N_STRIP, late_send, 0)

    def source(n):
        return shift(place, 0, acq_back(acq_step(n)))[0]

    def edge_copy(n, up):
        a = source(n)
        to = (strip + (1 if up else N_STRIP - 1)) % N_STRIP
        return pltpu.make_async_remote_copy(
            src_ref=edges_ref.at[a],
            dst_ref=(before_ref if up else after_ref).at[a],
            send_sem=edge_send.at[1 if up else 0, n],
            recv_sem=edge_recv.at[1 if up else 0, n],
            device_id=device((acq, to)),
            device_id_type=mesh_id,
        )

    has_before = jnp.where(strip > 0, 1.0, 0.0)
    has_after = jnp.where(strip < N_STRIP - 1, 1.0, 0.0)

    def block(n, carry):
        @pl.when(n < N_GROUP)
        def _():
            a = source(n)

            @pl.when(n == 0)
            def _():
                own.wait()

            def arrive(i, carry):
                @pl.when(n * N_STRIP + i > 0)
                def _():
                    slot_copy(n, i).wait_recv()

                return carry

            lax.fori_loop(0, N_STRIP, arrive, 0)
            slots = slots_ref[a].astype(jnp.float32).reshape(N_STRIP * CAP, PIECE).astype(jnp.bfloat16)
            rows_ref[n % 2] = slots
            edges_ref[a] = edge_rows(slots)
            edge_copy(n, True).start()
            edge_copy(n, False).start()

        @pl.when(n > 0)
        def _():
            edge_copy(n - 1, True).wait_recv()
            edge_copy(n - 1, False).wait_recv()
            a = source(n - 1)
            at = pl.ds(pl.multiple_of(a * 16, 16), 16)

            def store(o, part, cols, value):
                win_ref[o, part, cols, at, :] = value

            regroup(
                rows_ref[(n + 1) % 2], before_ref[a], after_ref[a], has_before, has_after, lines_ref, store
            )

        return carry

    lax.fori_loop(0, N_GROUP + 1, block, 0)

    def code_copy(n, o):
        to = shift(place, 0, acq_step(n))
        return pltpu.make_async_remote_copy(
            src_ref=code_ref.at[o, to[0]],
            dst_ref=out_ref.at[acq, o],
            send_sem=code_send.at[n, o],
            recv_sem=code_recv.at[n, o],
            device_id=device(to),
            device_id_type=mesh_id,
        )

    def code_keep(o):
        return pltpu.make_async_copy(code_ref.at[o, acq], out_ref.at[acq, o], code_own.at[o])

    def line(o, carry):
        def store(q, code_real, code_imag):
            code_ref[o, :, q, :, 0:128] = code_real
            code_ref[o, :, q, :, 128:256] = code_imag

        gram(win_ref, mask_ref, o, store)
        for n in range(1, N_GROUP):
            code_copy(n, o).start()
        code_keep(o).start()
        return carry

    lax.fori_loop(0, 8, line, 0)

    def finish(o, carry):
        code_keep(o).wait()
        for n in range(1, N_GROUP):
            code_copy(n, o).wait()
        return carry

    lax.fori_loop(0, 8, finish, 0)

    def sent(j, carry):
        slot_copy(j // N_STRIP, j % N_STRIP).wait_send()
        return carry

    lax.fori_loop(1, N_GROUP * N_STRIP, sent, 0)

    def edge_sent(n, carry):
        edge_copy(n, True).wait_send()
        edge_copy(n, False).wait_send()
        return carry

    lax.fori_loop(0, N_GROUP, edge_sent, 0)


def place_kernel(code_ref, out_ref, flat_ref, power_ref):
    m = pl.program_id(0)

    @pl.when(m == 0)
    def _():
        for o in range(8):
            for g in range(8):
                at = (o * 64 + g * 8) * 16
                block = code_ref[g, o * 8 : o * 8 + 8].astype(jnp.float32)
                block = block.reshape(128, 256)
                flat_ref[0, at : at + 128, :] = block[:, :128]
                flat_ref[1, at : at + 128, :] = block[:, 128:]
        high = flat_ref[0, pl.ds(15, 512, stride=16), :]
        rest = flat_ref[1, pl.ds(15, 512, stride=16), :]
        power_ref[...] = (high + rest).T

    power_n = power_ref[...]
    me = lax.axis_index("acq") * 16 + m
    power_m = power_ref[pl.ds(me, 1), :]
    scale = jnp.sqrt(power_n) * jnp.sqrt(power_m) * lax.rsqrt(power_n * power_m + epsilon)
    for part in range(2):
        codes = flat_ref[part, pl.ds(m, 512, stride=16), :].T
        scaled = jnp.log2(codes) * (1.0 / CODE) * scale
        for block in range(8):
            for t in range(4):
                piece = scaled[block * 16 : block * 16 + ACQ_LOC, t * 128 : t * 128 + 128]
                out_ref[0, pl.ds(block * ACQ_LOC * 8 + t * 2 + part, ACQ_LOC, stride=8), :] = piece


def per_device(
    raw_echo_values,
    cell_target_line,
    cell_track_displacement,
    along_track_chirp_slope,
    along_track_look_radius,
    range_look_radius,
):
    f32, bf16 = jnp.float32, jnp.bfloat16
    squared = cell_track_displacement[0].astype(f32) ** 2
    phase = squared[..., None] * along_track_chirp_slope
    line = cell_target_line[0].astype(f32)[..., None]
    gap = jnp.zeros((N_STRIP, CAP, 64 - ACQ_LOC), f32)
    ramp = jnp.concatenate([jnp.cos(phase), gap, jnp.sin(phase), gap[..., 1:], line], axis=-1)
    raw = raw_echo_values.reshape(N_STRIP, CAP, ACQ_LOC, 2, 4, 128)
    raw = raw.transpose(0, 1, 2, 4, 3, 5).reshape(N_STRIP, CAP * ACQ_LOC * 8, 128)
    group = lax.axis_index("acq")
    radius = lax.dynamic_slice_in_dim(range_look_radius, group * 8, 8, 0)
    across = jnp.arange(16, dtype=jnp.int32)[None, :] - 8
    col_mask = (jnp.abs(across) <= radius[:, None]).reshape(8, 2, 8)
    row_mask = jnp.abs(across) <= along_track_look_radius[:, None]
    masks = (row_mask[:, None, None, None, :] & col_mask[None, :, :, :, None]).reshape(8, 16, 128).astype(bf16)
    dma = pltpu.SemaphoreType.DMA
    received = pl.pallas_call(
        stack_kernel,
        out_shape=jax.ShapeDtypeStruct((N_GROUP, 8, 8, 16, 256), bf16),
        in_specs=[
            pl.BlockSpec(memory_space=pl.ANY),
            pl.BlockSpec(memory_space=pltpu.VMEM),
            pl.BlockSpec(memory_space=pltpu.VMEM),
        ],
        out_specs=pl.BlockSpec(memory_space=pl.ANY),
        scratch_shapes=[
            pltpu.VMEM((N_STRIP, CAP * ACQ_LOC * 8, 128), f32),
            pltpu.VMEM((N_GROUP, N_STRIP, CAP, PIECE), bf16),
            pltpu.VMEM((N_GROUP, N_STRIP, CAP, PIECE), bf16),
            pltpu.VMEM((2, N_STRIP * CAP, PIECE), bf16),
            pltpu.VMEM((N_GROUP, 16, PIECE), bf16),
            pltpu.VMEM((N_GROUP, 16, PIECE), bf16),
            pltpu.VMEM((N_GROUP, 16, PIECE), bf16),
            pltpu.VMEM((PIECE, 128), f32),
            pltpu.VMEM((8, 2, 9, 128, 128), bf16),
            pltpu.VMEM((8, N_GROUP, 8, 16, 256), bf16),
            dma((N_STRIP,)),
            dma((N_GROUP * N_STRIP,)),
            dma((N_GROUP * N_STRIP,)),
            dma,
            dma((2, N_GROUP)),
            dma((2, N_GROUP)),
            dma((N_GROUP, 8)),
            dma((N_GROUP, 8)),
            dma((8,)),
        ],
        compiler_params=pltpu.CompilerParams(vmem_limit_bytes=VMEM, collective_id=0, has_side_effects=True),
        name="stack",
    )(raw, ramp, masks)
    received = received.reshape(N_GROUP, 64, 16, 256)
    placed = pl.pallas_call(
        place_kernel,
        grid=(ACQ_LOC,),
        out_shape=jax.ShapeDtypeStruct((ACQ_LOC, 960, 128), f32),
        in_specs=[pl.BlockSpec((8, 64, 16, 256), lambda m: (0, 0, 0, 0))],
        out_specs=pl.BlockSpec((1, 960, 128), lambda m: (m, 0, 0)),
        scratch_shapes=[pltpu.VMEM((2, 512 * 16, 128), f32), pltpu.VMEM((128, 512), f32)],
        compiler_params=params(),
        name="place",
    )(received)
    placed = placed.reshape(ACQ_LOC, 120, 4, 2, 128).transpose(0, 1, 3, 2, 4)
    return placed.reshape(ACQ_LOC, 120, 2, 512)


def solution(mesh):
    placed = (
        P("strip", None, None, "acq", None, None),
        P("strip", None, None),
        P("strip", None, None),
        P("acq"),
        P("strip"),
        P(),
    )
    return jax.shard_map(
        per_device,
        mesh=mesh,
        in_specs=placed,
        out_specs=P("acq", None, None, "strip"),
        check_vma=False,
    )
```

time: 204 us -> 186 us (0.912)
  the two profiles are of different devices: /device:TPU:7 before, /device:TPU:1 now
where the time goes in v2:
time: 186 us; the launch traced here: 185 us
  Pallas kernels  179 us (96%)
  other arithmetic  3.81 us (2%)
  local copies, waits for them, and re-layouts  1.99 us (1%)
    pallas_call x1, Pallas kernels, per_device(): pl.pallas_call(stack_kernel, out_shape=jax.ShapeDtypeStruct((N_GROUP, 8,...  166 us
    pallas_call x1, Pallas kernels, per_device(): pl.pallas_call(place_kernel, grid=(ACQ_LOC,), out_shape=jax.ShapeDtypeStr...  12.6 us

profile of v2, /device:TPU:1, one launch (start us, length us, event | category | flops | bytes accessed | tf_op | source)
XLA Modules:
  0.0 184.8 jit_solution(17923140402057218608)
XLA Ops:
  0.0 0.7 dynamic_slice.3
  0.7 0.7 broadcast_compare_fusion.1
  1.5 0.1 broadcast_compare_fusion
  1.5 0.7 convert_bitcast_fusion
  2.2 0.7 multiply_bitcast_fusion
  2.9 0.1 copy.8
  3.0 0.1 and.24
  3.1 0.1 and.26
  3.2 0.1 and.27
  3.3 0.7 and_convert_fusion.mask_ref
  3.9 0.1 copy.9
  4.1 1.0 multiply_sine_fusion
  5.1 0.8 concatenate.3.ramp_ref
  5.8 166.4 %stack.1 = bf16[8,8,8,16,256]{4,3,2,1,0:T(8,128)(2,1)} custom-call(f32[16,960,128]{2,1,0:T(8,128)} %bitcast.18, f32[16,8,128]{2,1,0:T(8,128)} %concatenate.3.ramp_ref, bf16[8,16,128]{2,1,0:T(8,128)(2,1)} %and_convert_fusion.mask_ref), custom_call_target="tpu_custom_call" | custom-call | tf_op jit(solution)/shard_map/stack/pallas_call | solution.py:409
  172.2 12.6 %place.1 = f32[15,960,128]{2,1,0:T(8,128)} custom-call(bf16[8,64,16,256]{3,2,1,0:T(8,128)(2,1)} %bitcast.17), custom_call_target="tpu_custom_call" | custom-call | tf_op jit(solution)/shard_map/place/pallas_call | solution.py:443
  (5 shorter events, 0.0 us)

commit v3 on v2

--- a/solution.py
+++ b/solution.py
@@ -11,7 +11,8 @@
 CAP = 8
 ACQ_LOC = 15
 PIECE = 2176
-ROW_LANE = 2160
+ROW_LANE = 2168
+PLACE = 3
 CODE = 120.0
 VMEM = 56 * 1024 * 1024
 
@@ -48,44 +49,46 @@
     return ((4 - step // 2) % 4) * 2 + step % 2
 
 
-def pack_tile(raw_ref, ramp_ref, packed_ref, s, t):
-    ramp = ramp_ref[s]
+def pack_strip(raw_ref, packed_ref, s, line, phase):
+    cosines, sines = jnp.cos(phase), jnp.sin(phase)
     lane = lax.broadcasted_iota(jnp.int32, (CAP, 128), 1)
-    low = lane < 64
-    left_tile, right_tile = (t + 3) % 4, (t + 1) % 4
-    kept = jnp.where(low, jnp.where(t < 3, 1.0, 0.0), jnp.where(t > 0, 1.0, 0.0))
-    zero = jnp.zeros((CAP, 128), jnp.float32)
-    line = jnp.where(lane == ROW_LANE - 2048, ramp[:, 127:128], 0.0)
-    halo = [[zero, line], [zero, line]]
-
-    def load(a, tile, part):
-        return raw_ref[s, pl.ds(a * 8 + tile * 2 + part, CAP, stride=ACQ_LOC * 8), :]
-
+    lane16 = lax.broadcasted_iota(jnp.int32, (2 * CAP, 128), 1)
+    low, low16 = lane < 64, lane16 < 64
+    halo = [jnp.zeros((2 * CAP, 128), jnp.bfloat16) for _ in range(N_GROUP)]
     for a in range(ACQ_LOC):
-        cosine = jnp.broadcast_to(ramp[:, a : a + 1], (CAP, 128))
-        sine = jnp.broadcast_to(ramp[:, 64 + a : 65 + a], (CAP, 128))
-        real, imag = load(a, t, 0), load(a, t, 1)
-        main = [real * cosine + imag * sine, imag * cosine - real * sine]
-        real = jnp.where(low, load(a, right_tile, 0), load(a, left_tile, 0)) * kept
-        imag = jnp.where(low, load(a, right_tile, 1), load(a, left_tile, 1)) * kept
-        outer = [real * cosine + imag * sine, imag * cosine - real * sine]
-        even = jnp.where(low, main[0], pltpu.roll(main[1], 64, 1))
-        odd = jnp.where(low, pltpu.roll(main[0], 64, 1), main[1])
-        packed_ref[2 * t, s, :, a * 128 : a * 128 + 128] = even.astype(jnp.bfloat16)
-        packed_ref[2 * t + 1, s, :, a * 128 : a * 128 + 128] = odd.astype(jnp.bfloat16)
-        vreg = a // 8
+        cosine = jnp.broadcast_to(cosines[:, a : a + 1], (CAP, 128))
+        sine = jnp.broadcast_to(sines[:, a : a + 1], (CAP, 128))
+        tiles = []
+        for t in range(4):
+            row = a * 8 + t * 2
+            real = raw_ref[s, pl.ds(row, CAP, stride=ACQ_LOC * 8), :]
+            imag = raw_ref[s, pl.ds(row + 1, CAP, stride=ACQ_LOC * 8), :]
+            new_real = real * cosine + imag * sine
+            new_imag = imag * cosine - real * sine
+            tiles.append(jnp.concatenate([new_real, new_imag], axis=0).astype(jnp.bfloat16))
+            even = jnp.where(low, new_real, pltpu.roll(new_imag, 64, 1))
+            odd = jnp.where(low, pltpu.roll(new_real, 64, 1), new_imag)
+            packed_ref[2 * t, s, :, a * 128 : a * 128 + 128] = even.astype(jnp.bfloat16)
+            packed_ref[2 * t + 1, s, :, a * 128 : a * 128 + 128] = odd.astype(jnp.bfloat16)
+        left = (lane16 >= a * 8) & (lane16 < a * 8 + 4)
+        right = (lane16 >= a * 8 + 4) & (lane16 < a * 8 + 8)
+        for bound in range(1, N_GROUP):
+            t = bound // 2
+            if bound % 2:
+                source, start = tiles[t], 60
+            else:
+                source, start = jnp.where(low16, tiles[t], tiles[t - 1]), 124
+            moved = pltpu.roll(source, (a * 8 - start) % 128, 1)
+            halo[bound] = jnp.where(left, moved, halo[bound])
+            halo[bound - 1] = jnp.where(right, moved, halo[bound - 1])
+    for group in range(N_GROUP):
+        both = halo[group].astype(jnp.float32)
         for part in range(2):
-            base = (a % 8) * 16 + part * 8
-            left = (lane >= base) & (lane < base + 4)
-            right = (lane >= base + 4) & (lane < base + 8)
-            inner = pltpu.roll(main[part], (base - 60) % 128, 1)
-            edge = pltpu.roll(outer[part], (base - 124) % 128, 1)
-            halo[0][vreg] = jnp.where(left, edge, jnp.where(right, inner, halo[0][vreg]))
-            halo[1][vreg] = jnp.where(left, inner, jnp.where(right, edge, halo[1][vreg]))
-    for side in range(2):
-        for vreg in range(2):
-            at = ACQ_LOC * 128 + vreg * 128
-            packed_ref[2 * t + side, s, :, at : at + 128] = halo[side][vreg].astype(jnp.bfloat16)
+            at = ACQ_LOC * 128 + part * 128
+            rows = both[part * CAP : part * CAP + CAP]
+            if part:
+                rows = jnp.where(lane == ROW_LANE - at, line, rows)
+            packed_ref[group, s, :, at : at + 128] = rows.astype(jnp.bfloat16)
 
 
 def edge_rows(slots):
@@ -126,30 +129,31 @@
                 if 0 <= col < 64:
                     at, step = part * 64 + col, 128
                 else:
-                    at, step = ACQ_LOC * 128 + part * 8 + c, 16
+                    at, step = ACQ_LOC * 128 + part * 128 + c, 8
                 v.append(lines_ref[pl.ds(at, 16, stride=step), :].astype(jnp.bfloat16))
+            v = [pltpu.roll(v[i], 16 * i, 1) if i else v[i] for i in range(8)]
+            v = [v[-i % 8] for i in range(8)]
             for bit in (1, 2, 4):
-                clear = (group & bit) == 0
-                for i in range(8):
-                    if i & bit:
-                        continue
-                    a, b = v[i], v[i + bit]
-                    v[i] = jnp.where(clear, a, pltpu.roll(b, 16 * bit, 1))
-                    v[i + bit] = jnp.where(clear, pltpu.roll(a, 128 - 16 * bit, 1), b)
+                moving = (group & bit) != 0
+                v = [jnp.where(moving, v[(i - bit) % 8], v[i]) for i in range(8)]
+            v = [pltpu.roll(v[i], 128 - 16 * i, 1) if i else v[i] for i in range(8)]
             for o in range(8):
                 store(o, part, block, v[o])
 
 
-def gram(win_ref, mask_ref, o, store):
+def gram(win_ref, row_radius, col_radius, o, store):
     row = lax.broadcasted_iota(jnp.int32, (128, 128), 0)
     col = lax.broadcasted_iota(jnp.int32, (128, 128), 1)
     diagonal = row == col
     spare = row % 16 == 15
     dims = (((1,), (1,)), ((), ()))
+    lane = lax.broadcasted_iota(jnp.int32, (1, 256), 1)
+    row_mask = (jnp.abs(lane % 16 - 8) <= row_radius).astype(jnp.float32)
     for q in range(8):
         re = jnp.concatenate([win_ref[o, 0, q], win_ref[o, 0, q + 1]], axis=1)
         im = jnp.concatenate([win_ref[o, 1, q], win_ref[o, 1, q + 1]], axis=1)
-        mask = jnp.concatenate([mask_ref[o, 2 * q : 2 * q + 1, :], mask_ref[o, 2 * q + 1 : 2 * q + 2, :]], axis=1)
+        mask = (jnp.abs(lane // 16 - 8) <= col_radius(q)).astype(jnp.float32)
+        mask = (mask * row_mask).astype(jnp.bfloat16)
         left = jnp.concatenate([re * mask, im * mask], axis=1)
         real = lax.dot_general(left, jnp.concatenate([re, im], axis=1), dims, preferred_element_type=jnp.float32)
         imag = lax.dot_general(left, jnp.concatenate([-im, re], axis=1), dims, preferred_element_type=jnp.float32)
@@ -165,7 +169,7 @@
 
 
 def stack_kernel(
-    raw_hbm, ramp_ref, mask_ref, out_ref,
+    raw_hbm, line_ref, offset_ref, slope_ref, row_radius_ref, col_radius_ref, out_ref,
     raw_ref, packed_ref, slots_ref, rows_ref, edges_ref, before_ref, after_ref, lines_ref, win_ref, code_ref,
     raw_sem, send_sem, recv_sem, own_sem, edge_send, edge_recv, code_send, code_recv, code_own,
 ):
@@ -194,6 +198,20 @@
         return carry
 
     lax.fori_loop(0, N_STRIP, fetch_start, 0)
+    squared = offset_ref[...].astype(jnp.float32) ** 2
+    lines = line_ref[...].astype(jnp.float32)
+    reader_lane = lax.broadcasted_iota(jnp.int32, (CAP, N_STRIP), 1)
+
+    def pack(i, carry):
+        s = shift(place, strip_step(i), 0)[1]
+        fetch(s).wait()
+        mine = reader_lane == s
+        column = jnp.sum(jnp.where(mine, squared, 0.0), axis=1, keepdims=True)
+        line = jnp.sum(jnp.where(mine, lines, 0.0), axis=1, keepdims=True)
+        pack_strip(raw_ref, packed_ref, s, line, column * slope_ref[...])
+        return carry
+
+    lax.fori_loop(0, N_STRIP, pack, 0)
     pl.semaphore_wait(barrier, N_STRIP * N_GROUP - 1)
 
     own = pltpu.make_async_copy(packed_ref.at[acq, strip], slots_ref.at[acq, strip], own_sem)
@@ -214,37 +232,15 @@
         def _():
             slot_copy(n, i).start()
 
-    y = acq // 2
-
-    def early(i, carry):
-        s = shift(place, strip_step(i), 0)[1]
-        fetch(s).wait()
-        pack_tile(raw_ref, ramp_ref, packed_ref, s, y)
-        pack_tile(raw_ref, ramp_ref, packed_ref, s, (y + 2) % 4)
-
-        @pl.when(i == 0)
-        def _():
-            own.start()
-
-        for n in range(4):
-            send(n, i)
-        return carry
-
-    lax.fori_loop(0, N_STRIP, early, 0)
-
-    def late(i, carry):
-        s = shift(place, strip_step(i), 0)[1]
-        pack_tile(raw_ref, ramp_ref, packed_ref, s, (y + 1) % 4)
-        pack_tile(raw_ref, ramp_ref, packed_ref, s, (y + 3) % 4)
-        return carry
-
-    lax.fori_loop(0, N_STRIP, late, 0)
-
-    def late_send(j, carry):
-        send(4 + j // N_STRIP, j % N_STRIP)
-        return carry
-
-    lax.fori_loop(0, 4 * N_STRIP, late_send, 0)
+    own.start()
+    for some in ((0, 1, 2, 3), (4, 5), (6, 7)):
+
+        def send_some(i, carry):
+            for n in some:
+                send(n, i)
+            return carry
+
+        lax.fori_loop(0, N_STRIP, send_some, 0)
 
     def source(n):
         return shift(place, 0, acq_back(acq_step(n)))[0]
@@ -324,7 +320,7 @@
             code_ref[o, :, q, :, 0:128] = code_real
             code_ref[o, :, q, :, 128:256] = code_imag
 
-        gram(win_ref, mask_ref, o, store)
+        gram(win_ref, row_radius_ref[o], lambda q: col_radius_ref[acq * 8 + q], o, store)
         for n in range(1, N_GROUP):
             code_copy(n, o).start()
         code_keep(o).start()
@@ -355,9 +351,9 @@
 
 
 def place_kernel(code_ref, out_ref, flat_ref, power_ref):
-    m = pl.program_id(0)
-
-    @pl.when(m == 0)
+    step = pl.program_id(0)
+
+    @pl.when(step == 0)
     def _():
         for o in range(8):
             for g in range(8):
@@ -371,16 +367,19 @@
         power_ref[...] = (high + rest).T
 
     power_n = power_ref[...]
-    me = lax.axis_index("acq") * 16 + m
-    power_m = power_ref[pl.ds(me, 1), :]
-    scale = jnp.sqrt(power_n) * jnp.sqrt(power_m) * lax.rsqrt(power_n * power_m + epsilon)
-    for part in range(2):
-        codes = flat_ref[part, pl.ds(m, 512, stride=16), :].T
-        scaled = jnp.log2(codes) * (1.0 / CODE) * scale
-        for block in range(8):
-            for t in range(4):
-                piece = scaled[block * 16 : block * 16 + ACQ_LOC, t * 128 : t * 128 + 128]
-                out_ref[0, pl.ds(block * ACQ_LOC * 8 + t * 2 + part, ACQ_LOC, stride=8), :] = piece
+    root_n = jnp.sqrt(power_n)
+    for j in range(PLACE):
+        m = step * PLACE + j
+        me = lax.axis_index("acq") * 16 + m
+        power_m = power_ref[pl.ds(me, 1), :]
+        scale = root_n * jnp.sqrt(power_m) * lax.rsqrt(power_n * power_m + epsilon) * (1.0 / CODE)
+        for part in range(2):
+            codes = flat_ref[part, pl.ds(m, 512, stride=16), :].T
+            scaled = jnp.log2(codes) * scale
+            for block in range(8):
+                for t in range(4):
+                    piece = scaled[block * 16 : block * 16 + ACQ_LOC, t * 128 : t * 128 + 128]
+                    out_ref[j, pl.ds(block * ACQ_LOC * 8 + t * 2 + part, ACQ_LOC, stride=8), :] = piece
 
 
 def per_device(
@@ -392,19 +391,8 @@
     range_look_radius,
 ):
     f32, bf16 = jnp.float32, jnp.bfloat16
-    squared = cell_track_displacement[0].astype(f32) ** 2
-    phase = squared[..., None] * along_track_chirp_slope
-    line = cell_target_line[0].astype(f32)[..., None]
-    gap = jnp.zeros((N_STRIP, CAP, 64 - ACQ_LOC), f32)
-    ramp = jnp.concatenate([jnp.cos(phase), gap, jnp.sin(phase), gap[..., 1:], line], axis=-1)
     raw = raw_echo_values.reshape(N_STRIP, CAP, ACQ_LOC, 2, 4, 128)
     raw = raw.transpose(0, 1, 2, 4, 3, 5).reshape(N_STRIP, CAP * ACQ_LOC * 8, 128)
-    group = lax.axis_index("acq")
-    radius = lax.dynamic_slice_in_dim(range_look_radius, group * 8, 8, 0)
-    across = jnp.arange(16, dtype=jnp.int32)[None, :] - 8
-    col_mask = (jnp.abs(across) <= radius[:, None]).reshape(8, 2, 8)
-    row_mask = jnp.abs(across) <= along_track_look_radius[:, None]
-    masks = (row_mask[:, None, None, None, :] & col_mask[None, :, :, :, None]).reshape(8, 16, 128).astype(bf16)
     dma = pltpu.SemaphoreType.DMA
     received = pl.pallas_call(
         stack_kernel,
@@ -413,6 +401,9 @@
             pl.BlockSpec(memory_space=pl.ANY),
             pl.BlockSpec(memory_space=pltpu.VMEM),
             pl.BlockSpec(memory_space=pltpu.VMEM),
+            pl.BlockSpec(memory_space=pltpu.VMEM),
+            pl.BlockSpec(memory_space=pltpu.SMEM),
+            pl.BlockSpec(memory_space=pltpu.SMEM),
         ],
         out_specs=pl.BlockSpec(memory_space=pl.ANY),
         scratch_shapes=[
@@ -438,14 +429,21 @@
         ],
         compiler_params=pltpu.CompilerParams(vmem_limit_bytes=VMEM, collective_id=0, has_side_effects=True),
         name="stack",
-    )(raw, ramp, masks)
+    )(
+        raw,
+        cell_target_line[0].T,
+        cell_track_displacement[0].T,
+        along_track_chirp_slope[None],
+        along_track_look_radius,
+        range_look_radius,
+    )
     received = received.reshape(N_GROUP, 64, 16, 256)
     placed = pl.pallas_call(
         place_kernel,
-        grid=(ACQ_LOC,),
+        grid=(ACQ_LOC // PLACE,),
         out_shape=jax.ShapeDtypeStruct((ACQ_LOC, 960, 128), f32),
         in_specs=[pl.BlockSpec((8, 64, 16, 256), lambda m: (0, 0, 0, 0))],
-        out_specs=pl.BlockSpec((1, 960, 128), lambda m: (m, 0, 0)),
+        out_specs=pl.BlockSpec((PLACE, 960, 128), lambda m: (m, 0, 0)),
         scratch_shapes=[pltpu.VMEM((2, 512 * 16, 128), f32), pltpu.VMEM((128, 512), f32)],
         compiler_params=params(),
         name="place",

time: 186 us -> 159 us (0.85)
  Pallas kernels: 179 us -> 157 us
  other arithmetic: 3.81 us -> 0 us
  local copies, waits for them, and re-layouts: 1.99 us -> 0 us
    pallas_call x1, Pallas kernels: 166 us -> 147 us  [per_device(): pl.pallas_call(stack_kernel, out_shape=jax.ShapeDtypeStruct((N_GROUP, 8,...]
    pallas_call x1, Pallas kernels: 12.6 us -> 9.72 us  [per_device(): pl.pallas_call(place_kernel, grid=(ACQ_LOC // PLACE,), out_shape=jax.Shap...]
where the time goes in v3:
time: 159 us; the launch traced here: 157 us
  Pallas kernels  157 us (99%)
    pallas_call x1, Pallas kernels, per_device(): pl.pallas_call(stack_kernel, out_shape=jax.ShapeDtypeStruct((N_GROUP, 8,...  147 us
    pallas_call x1, Pallas kernels, per_device(): pl.pallas_call(place_kernel, grid=(ACQ_LOC // PLACE,), out_shape=jax.Shap...  9.72 us

profile of v3, /device:TPU:1, one launch (start us, length us, event | category | flops | bytes accessed | tf_op | source)
XLA Modules:
  0.0 156.8 jit_solution(16348624523147024291)
XLA Ops:
  0.0 147.1 %stack.1 = bf16[8,8,8,16,256]{4,3,2,1,0:T(8,128)(2,1)} custom-call(f32[16,960,128]{2,1,0:T(8,128)} %bitcast.19, s32[8,16]{1,0:T(8,128)} %bitcast.20, s32[8,16]{1,0:T(8,128)} %bitcast.21, f32[1,15]{1,0:T(1,128)} %bitcast.22, s32[8]{0:T(128)} %row_radius_ref.1, s32[64]{0:T(128)} %col_radius_ref.1), custom_call_target="tpu_custom_call" | custom-call | tf_op jit(solution)/shard_map/stack/pallas_call | solution.py:397
  147.1 9.7 %place.1 = f32[15,960,128]{2,1,0:T(8,128)} custom-call(bf16[8,64,16,256]{3,2,1,0:T(8,128)(2,1)} %bitcast.18), custom_call_target="tpu_custom_call" | custom-call | tf_op jit(solution)/shard_map/place/pallas_call | solution.py:441

commit v4 on v3

--- a/solution.py
+++ b/solution.py
@@ -12,6 +12,7 @@
 ACQ_LOC = 15
 PIECE = 2176
 ROW_LANE = 2168
+EARLY = 8
 PLACE = 3
 CODE = 120.0
 VMEM = 56 * 1024 * 1024
@@ -39,9 +40,9 @@
 
 
 def acq_step(n):
-    half, rest = n // 4, n % 4
-    dy = (1 - half) * (rest // 2) * 2 + half * (1 + 2 * (rest % 2))
-    dh = (1 - half) * (rest % 2) + half * (rest // 2)
+    far, second, odd = n // 4, (n // 2) % 2, n % 2
+    dy = far + 2 * ((second + odd) % 2)
+    dh = (second + odd) % 2 + (1 - 2 * ((second + odd) % 2)) * second
     return dy * 2 + dh
 
 
@@ -103,24 +104,29 @@
     return (total * inverse).astype(jnp.bfloat16)
 
 
-def regroup(slots, before, after, has_before, has_after, lines_ref, store):
+def window_picks(slots):
     line = slots[:, ROW_LANE : ROW_LANE + 1].astype(jnp.float32)
     lane = lax.broadcasted_iota(jnp.int32, (128, 128), 1)
     row = 8 * (lane // 16) + lane % 16 - 4
     inside = (row >= 0) & (row < 64)
-    pick = (line == jnp.where(inside, row, 1000).astype(jnp.float32)).astype(jnp.float32)
-    lane16 = lax.broadcasted_iota(jnp.int32, (16, 128), 1)
-    sub16 = lax.broadcasted_iota(jnp.int32, (16, 128), 0)
-    pick_before = ((lane16 < 4) & (sub16 == lane16 + 4)).astype(jnp.float32) * has_before
-    pick_after = ((lane16 >= 124) & (sub16 == lane16 - 124)).astype(jnp.float32) * has_after
-    picks = jnp.concatenate([pick, pick_before, pick_after], axis=0)
+    return (line == jnp.where(inside, row, 1000).astype(jnp.float32)).astype(jnp.float32)
+
+
+def border_picks(has_before, has_after):
+    lane = lax.broadcasted_iota(jnp.int32, (32, 128), 1)
+    sub = lax.broadcasted_iota(jnp.int32, (32, 128), 0)
+    before = ((lane < 4) & (sub == lane + 4)).astype(jnp.float32) * has_before
+    after = ((lane >= 124) & (sub == lane - 108)).astype(jnp.float32) * has_after
+    return before + after
+
+
+def regroup(rows, picks, lines_ref, store):
     inverse = 1.0 / jnp.maximum(jnp.sum(picks, axis=0, keepdims=True), 1.0)
-    rows = jnp.concatenate([slots, before, after], axis=0)
     total = lax.dot_general(
         rows, picks.astype(jnp.bfloat16), (((0,), (0,)), ((), ())), preferred_element_type=jnp.float32
     )
     lines_ref[...] = total * inverse
-    group = lane16 // 16
+    group = lax.broadcasted_iota(jnp.int32, (16, 128), 1) // 16
     for part in range(2):
         for block in range(9):
             v = []
@@ -136,9 +142,11 @@
             for bit in (1, 2, 4):
                 moving = (group & bit) != 0
                 v = [jnp.where(moving, v[(i - bit) % 8], v[i]) for i in range(8)]
-            v = [pltpu.roll(v[i], 128 - 16 * i, 1) if i else v[i] for i in range(8)]
-            for o in range(8):
-                store(o, part, block, v[o])
+            store(part, block, v)
+
+
+def turned(value, o):
+    return pltpu.roll(value, 128 - 16 * o, 1) if o else value
 
 
 def gram(win_ref, row_radius, col_radius, o, store):
@@ -170,8 +178,8 @@
 
 def stack_kernel(
     raw_hbm, line_ref, offset_ref, slope_ref, row_radius_ref, col_radius_ref, out_ref,
-    raw_ref, packed_ref, slots_ref, rows_ref, edges_ref, before_ref, after_ref, lines_ref, win_ref, code_ref,
-    raw_sem, send_sem, recv_sem, own_sem, edge_send, edge_recv, code_send, code_recv, code_own,
+    raw_ref, packed_ref, slots_ref, edges_ref, before_ref, after_ref, lines_ref, win_ref, code_ref,
+    group_sem, raw_sem, send_sem, recv_sem, own_sem, edge_send, edge_recv, code_send, code_recv, code_own,
 ):
     acq, strip = lax.axis_index("acq"), lax.axis_index("strip")
     place = (acq, strip)
@@ -182,13 +190,13 @@
 
     barrier = pltpu.get_barrier_semaphore()
 
-    def greet(i, carry):
-        pl.semaphore_signal(
-            barrier, inc=1, device_id=device(shift(place, i % N_STRIP, i // N_STRIP)), device_id_type=mesh_id
-        )
-        return carry
-
-    lax.fori_loop(1, N_STRIP * N_GROUP, greet, 0)
+    def greet(semaphore, to):
+        pl.semaphore_signal(semaphore, inc=1, device_id=device(to), device_id_type=mesh_id)
+
+    for i in range(1, N_STRIP):
+        greet(barrier, shift(place, i, 0))
+    for n in range(1, N_GROUP):
+        greet(barrier, shift(place, 0, n))
 
     def fetch(s):
         return pltpu.make_async_copy(raw_hbm.at[s], raw_ref.at[s], raw_sem.at[s])
@@ -211,8 +219,12 @@
         pack_strip(raw_ref, packed_ref, s, line, column * slope_ref[...])
         return carry
 
-    lax.fori_loop(0, N_STRIP, pack, 0)
-    pl.semaphore_wait(barrier, N_STRIP * N_GROUP - 1)
+    lax.fori_loop(0, 2, pack, 0)
+    pl.semaphore_wait(barrier, N_STRIP + N_GROUP - 2)
+    for n in range(1, N_GROUP):
+        greet(group_sem, shift(place, 0, n))
+    lax.fori_loop(2, EARLY, pack, 0)
+    pl.semaphore_wait(group_sem, N_GROUP - 1)
 
     own = pltpu.make_async_copy(packed_ref.at[acq, strip], slots_ref.at[acq, strip], own_sem)
 
@@ -232,74 +244,69 @@
         def _():
             slot_copy(n, i).start()
 
+    def send_pair(first):
+        def body(i, carry):
+            send(first, i)
+            send(first + 1, i)
+            return carry
+
+        return body
+
+    def pack_and_send(i, carry):
+        pack(i, carry)
+        return send_pair(0)(i, carry)
+
+    lax.fori_loop(0, EARLY, send_pair(0), 0)
+    lax.fori_loop(EARLY, N_STRIP, pack_and_send, 0)
     own.start()
-    for some in ((0, 1, 2, 3), (4, 5), (6, 7)):
-
-        def send_some(i, carry):
-            for n in some:
-                send(n, i)
-            return carry
-
-        lax.fori_loop(0, N_STRIP, send_some, 0)
+    for first in (2, 4, 6):
+        lax.fori_loop(0, N_STRIP, send_pair(first), 0)
 
     def source(n):
         return shift(place, 0, acq_back(acq_step(n)))[0]
 
-    def edge_copy(n, up):
-        a = source(n)
+    def edge_copy(up):
         to = (strip + (1 if up else N_STRIP - 1)) % N_STRIP
         return pltpu.make_async_remote_copy(
-            src_ref=edges_ref.at[a],
-            dst_ref=(before_ref if up else after_ref).at[a],
-            send_sem=edge_send.at[1 if up else 0, n],
-            recv_sem=edge_recv.at[1 if up else 0, n],
+            src_ref=edges_ref,
+            dst_ref=before_ref if up else after_ref,
+            send_sem=edge_send.at[1 if up else 0],
+            recv_sem=edge_recv.at[1 if up else 0],
             device_id=device((acq, to)),
             device_id_type=mesh_id,
         )
 
-    has_before = jnp.where(strip > 0, 1.0, 0.0)
-    has_after = jnp.where(strip < N_STRIP - 1, 1.0, 0.0)
+    def rows_of(a):
+        return pl.ds(pl.multiple_of(a * 16, 16), 16)
 
     def block(n, carry):
-        @pl.when(n < N_GROUP)
+        a = source(n)
+
+        @pl.when(n == 0)
         def _():
-            a = source(n)
-
-            @pl.when(n == 0)
+            own.wait()
+
+        def arrive(i, carry):
+            @pl.when(n * N_STRIP + i > 0)
             def _():
-                own.wait()
-
-            def arrive(i, carry):
-                @pl.when(n * N_STRIP + i > 0)
-                def _():
-                    slot_copy(n, i).wait_recv()
-
-                return carry
-
-            lax.fori_loop(0, N_STRIP, arrive, 0)
-            slots = slots_ref[a].astype(jnp.float32).reshape(N_STRIP * CAP, PIECE).astype(jnp.bfloat16)
-            rows_ref[n % 2] = slots
-            edges_ref[a] = edge_rows(slots)
-            edge_copy(n, True).start()
-            edge_copy(n, False).start()
-
-        @pl.when(n > 0)
-        def _():
-            edge_copy(n - 1, True).wait_recv()
-            edge_copy(n - 1, False).wait_recv()
-            a = source(n - 1)
-            at = pl.ds(pl.multiple_of(a * 16, 16), 16)
-
-            def store(o, part, cols, value):
-                win_ref[o, part, cols, at, :] = value
-
-            regroup(
-                rows_ref[(n + 1) % 2], before_ref[a], after_ref[a], has_before, has_after, lines_ref, store
-            )
-
-        return carry
-
-    lax.fori_loop(0, N_GROUP + 1, block, 0)
+                slot_copy(n, i).wait_recv()
+
+            return carry
+
+        lax.fori_loop(0, N_STRIP, arrive, 0)
+        slots = slots_ref[a].astype(jnp.float32).reshape(N_STRIP * CAP, PIECE).astype(jnp.bfloat16)
+        edges_ref[a] = edge_rows(slots)
+
+        def store(part, cols, value):
+            for o in range(8):
+                win_ref[o, part, cols, rows_of(a), :] = turned(value[o], o)
+
+        regroup(slots, window_picks(slots), lines_ref, store)
+        return carry
+
+    lax.fori_loop(0, N_GROUP, block, 0)
+    edge_copy(True).start()
+    edge_copy(False).start()
 
     def code_copy(n, o):
         to = shift(place, 0, acq_step(n))
@@ -326,7 +333,23 @@
         code_keep(o).start()
         return carry
 
-    lax.fori_loop(0, 8, line, 0)
+    lax.fori_loop(1, 7, line, 0)
+
+    edge_copy(True).wait_recv()
+    edge_copy(False).wait_recv()
+    picks = border_picks(jnp.where(strip > 0, 1.0, 0.0), jnp.where(strip < N_STRIP - 1, 1.0, 0.0))
+
+    def border(a, carry):
+        def store(part, cols, value):
+            for o in (0, 7):
+                win_ref[o, part, cols, rows_of(a), :] += turned(value[o], o)
+
+        regroup(jnp.concatenate([before_ref[a], after_ref[a]], axis=0), picks, lines_ref, store)
+        return carry
+
+    lax.fori_loop(0, N_GROUP, border, 0)
+    line(0, 0)
+    line(7, 0)
 
     def finish(o, carry):
         code_keep(o).wait()
@@ -342,12 +365,8 @@
 
     lax.fori_loop(1, N_GROUP * N_STRIP, sent, 0)
 
-    def edge_sent(n, carry):
-        edge_copy(n, True).wait_send()
-        edge_copy(n, False).wait_send()
-        return carry
-
-    lax.fori_loop(0, N_GROUP, edge_sent, 0)
+    edge_copy(True).wait_send()
+    edge_copy(False).wait_send()
 
 
 def place_kernel(code_ref, out_ref, flat_ref, power_ref):
@@ -410,19 +429,19 @@
             pltpu.VMEM((N_STRIP, CAP * ACQ_LOC * 8, 128), f32),
             pltpu.VMEM((N_GROUP, N_STRIP, CAP, PIECE), bf16),
             pltpu.VMEM((N_GROUP, N_STRIP, CAP, PIECE), bf16),
-            pltpu.VMEM((2, N_STRIP * CAP, PIECE), bf16),
             pltpu.VMEM((N_GROUP, 16, PIECE), bf16),
             pltpu.VMEM((N_GROUP, 16, PIECE), bf16),
             pltpu.VMEM((N_GROUP, 16, PIECE), bf16),
             pltpu.VMEM((PIECE, 128), f32),
             pltpu.VMEM((8, 2, 9, 128, 128), bf16),
             pltpu.VMEM((8, N_GROUP, 8, 16, 256), bf16),
+            pltpu.SemaphoreType.REGULAR,
             dma((N_STRIP,)),
             dma((N_GROUP * N_STRIP,)),
             dma((N_GROUP * N_STRIP,)),
             dma,
-            dma((2, N_GROUP)),
-            dma((2, N_GROUP)),
+            dma((2,)),
+            dma((2,)),
             dma((N_GROUP, 8)),
             dma((N_GROUP, 8)),
             dma((8,)),

time: 159 us -> 137 us (0.86); the launches traced: 157 us -> 137 us
  Pallas kernels: 157 us -> 137 us
    pallas_call x1, Pallas kernels: 147 us -> 127 us  [per_device(): pl.pallas_call(stack_kernel, out_shape=jax.ShapeDtypeStruct((N_GROUP, 8,...]
where the time goes in v4:
time: 137 us
  Pallas kernels  137 us (100%)
    pallas_call x1, Pallas kernels, per_device(): pl.pallas_call(stack_kernel, out_shape=jax.ShapeDtypeStruct((N_GROUP, 8,...  127 us
    pallas_call x1, Pallas kernels, per_device(): pl.pallas_call(place_kernel, grid=(ACQ_LOC // PLACE,), out_shape=jax.Shap...  9.72 us

profile of v4, /device:TPU:1, one launch (start us, length us, event | category | flops | bytes accessed | tf_op | source)
XLA Modules:
  0.0 137.2 jit_solution(283173438512135455)
XLA Ops:
  0.0 127.5 %stack.1 = bf16[8,8,8,16,256]{4,3,2,1,0:T(8,128)(2,1)} custom-call(f32[16,960,128]{2,1,0:T(8,128)} %bitcast.19, s32[8,16]{1,0:T(8,128)} %bitcast.20, s32[8,16]{1,0:T(8,128)} %bitcast.21, f32[1,15]{1,0:T(1,128)} %bitcast.22, s32[8]{0:T(128)} %row_radius_ref.1, s32[64]{0:T(128)} %col_radius_ref.1), custom_call_target="tpu_custom_call" | custom-call | tf_op jit(solution)/shard_map/stack/pallas_call | solution.py:416
  127.5 9.7 %place.1 = f32[15,960,128]{2,1,0:T(8,128)} custom-call(bf16[8,64,16,256]{3,2,1,0:T(8,128)(2,1)} %bitcast.18), custom_call_target="tpu_custom_call" | custom-call | tf_op jit(solution)/shard_map/place/pallas_call | solution.py:460

commit v5 on v4

--- a/solution.py
+++ b/solution.py
@@ -12,7 +12,7 @@
 ACQ_LOC = 15
 PIECE = 2176
 ROW_LANE = 2168
-EARLY = 8
+EARLY = 2
 PLACE = 3
 CODE = 120.0
 VMEM = 56 * 1024 * 1024
@@ -234,7 +234,7 @@
             src_ref=packed_ref.at[to[0], to[1]],
             dst_ref=slots_ref.at[acq, strip],
             send_sem=send_sem.at[n * N_STRIP + i],
-            recv_sem=recv_sem.at[n * N_STRIP + i],
+            recv_sem=recv_sem.at[n],
             device_id=device(to),
             device_id_type=mesh_id,
         )
@@ -279,23 +279,32 @@
     def rows_of(a):
         return pl.ds(pl.multiple_of(a * 16, 16), 16)
 
+    def arrival(n, a, count):
+        return pltpu.make_async_remote_copy(
+            src_ref=packed_ref.at[a, pl.ds(0, count)],
+            dst_ref=slots_ref.at[a, pl.ds(0, count)],
+            send_sem=send_sem.at[n],
+            recv_sem=recv_sem.at[n],
+            device_id=device((acq, (strip + 1) % N_STRIP)),
+            device_id_type=mesh_id,
+        )
+
+    def slots_of(a):
+        return slots_ref[a].astype(jnp.float32).reshape(N_STRIP * CAP, PIECE).astype(jnp.bfloat16)
+
     def block(n, carry):
         a = source(n)
 
         @pl.when(n == 0)
         def _():
             own.wait()
-
-        def arrive(i, carry):
-            @pl.when(n * N_STRIP + i > 0)
-            def _():
-                slot_copy(n, i).wait_recv()
-
-            return carry
-
-        lax.fori_loop(0, N_STRIP, arrive, 0)
-        slots = slots_ref[a].astype(jnp.float32).reshape(N_STRIP * CAP, PIECE).astype(jnp.bfloat16)
-        edges_ref[a] = edge_rows(slots)
+            arrival(n, a, N_STRIP - 1).wait_recv()
+
+        @pl.when(n > 0)
+        def _():
+            arrival(n, a, N_STRIP).wait_recv()
+
+        slots = slots_of(a)
 
         def store(part, cols, value):
             for o in range(8):
@@ -305,8 +314,6 @@
         return carry
 
     lax.fori_loop(0, N_GROUP, block, 0)
-    edge_copy(True).start()
-    edge_copy(False).start()
 
     def code_copy(n, o):
         to = shift(place, 0, acq_step(n))
@@ -333,7 +340,16 @@
         code_keep(o).start()
         return carry
 
-    lax.fori_loop(1, 7, line, 0)
+    line(1, 0)
+
+    def edge(a, carry):
+        edges_ref[a] = edge_rows(slots_of(a))
+        return carry
+
+    lax.fori_loop(0, N_GROUP, edge, 0)
+    edge_copy(True).start()
+    edge_copy(False).start()
+    lax.fori_loop(2, 7, line, 0)
 
     edge_copy(True).wait_recv()
     edge_copy(False).wait_recv()
@@ -351,22 +367,22 @@
     line(0, 0)
     line(7, 0)
 
-    def finish(o, carry):
+    def sent(j, carry):
+        slot_copy(j // N_STRIP, j % N_STRIP).wait_send()
+        return carry
+
+    lax.fori_loop(1, N_GROUP * N_STRIP, sent, 0)
+    edge_copy(True).wait_send()
+    edge_copy(False).wait_send()
+
+    def finish(j, carry):
+        o = (j + 1) % 7 + 6 * (j // 7)
         code_keep(o).wait()
         for n in range(1, N_GROUP):
             code_copy(n, o).wait()
         return carry
 
     lax.fori_loop(0, 8, finish, 0)
-
-    def sent(j, carry):
-        slot_copy(j // N_STRIP, j % N_STRIP).wait_send()
-        return carry
-
-    lax.fori_loop(1, N_GROUP * N_STRIP, sent, 0)
-
-    edge_copy(True).wait_send()
-    edge_copy(False).wait_send()
 
 
 def place_kernel(code_ref, out_ref, flat_ref, power_ref):
@@ -438,7 +454,7 @@
             pltpu.SemaphoreType.REGULAR,
             dma((N_STRIP,)),
             dma((N_GROUP * N_STRIP,)),
-            dma((N_GROUP * N_STRIP,)),
+            dma((N_GROUP,)),
             dma,
             dma((2,)),
             dma((2,)),

time: 137 us -> 134 us (0.978); the launches traced: 137 us -> 133 us
  Pallas kernels: 137 us -> 133 us
    pallas_call x1, Pallas kernels: 127 us -> 123 us  [per_device(): pl.pallas_call(stack_kernel, out_shape=jax.ShapeDtypeStruct((N_GROUP, 8,...]
where the time goes in v5:
time: 134 us; the launch traced here: 133 us
  Pallas kernels  133 us (99%)
    pallas_call x1, Pallas kernels, per_device(): pl.pallas_call(stack_kernel, out_shape=jax.ShapeDtypeStruct((N_GROUP, 8,...  123 us
    pallas_call x1, Pallas kernels, per_device(): pl.pallas_call(place_kernel, grid=(ACQ_LOC // PLACE,), out_shape=jax.Shap...  9.72 us

profile of v5, /device:TPU:1, one launch (start us, length us, event | category | flops | bytes accessed | tf_op | source)
XLA Modules:
  0.0 132.7 jit_solution(8587650339060179036)
XLA Ops:
  0.0 122.9 %stack.1 = bf16[8,8,8,16,256]{4,3,2,1,0:T(8,128)(2,1)} custom-call(f32[16,960,128]{2,1,0:T(8,128)} %bitcast.19, s32[8,16]{1,0:T(8,128)} %bitcast.20, s32[8,16]{1,0:T(8,128)} %bitcast.21, f32[1,15]{1,0:T(1,128)} %bitcast.22, s32[8]{0:T(128)} %row_radius_ref.1, s32[64]{0:T(128)} %col_radius_ref.1), custom_call_target="tpu_custom_call" | custom-call | tf_op jit(solution)/shard_map/stack/pallas_call | solution.py:432
  122.9 9.7 %place.1 = f32[15,960,128]{2,1,0:T(8,128)} custom-call(bf16[8,64,16,256]{3,2,1,0:T(8,128)(2,1)} %bitcast.18), custom_call_target="tpu_custom_call" | custom-call | tf_op jit(solution)/shard_map/place/pallas_call | solution.py:476

commit v6 on v5

--- a/solution.py
+++ b/solution.py
@@ -335,7 +335,7 @@
             code_ref[o, :, q, :, 128:256] = code_imag
 
         gram(win_ref, row_radius_ref[o], lambda q: col_radius_ref[acq * 8 + q], o, store)
-        for n in range(1, N_GROUP):
+        for n in (6, 1, 7, 2, 5, 3, 4):
             code_copy(n, o).start()
         code_keep(o).start()
         return carry
@@ -385,12 +385,19 @@
     lax.fori_loop(0, 8, finish, 0)
 
 
-def place_kernel(code_ref, out_ref, flat_ref, power_ref):
+def place_kernel(code_hbm, out_ref, flat_ref, power_ref, code_ref, code_sem):
     step = pl.program_id(0)
 
     @pl.when(step == 0)
     def _():
+        def fetch(o):
+            rows = pl.ds(o * 8, 8)
+            return pltpu.make_async_copy(code_hbm.at[:, rows], code_ref.at[:, rows], code_sem.at[o])
+
         for o in range(8):
+            fetch(o).start()
+        for o in range(8):
+            fetch(o).wait()
             for g in range(8):
                 at = (o * 64 + g * 8) * 16
                 block = code_ref[g, o * 8 : o * 8 + 8].astype(jnp.float32)
@@ -477,9 +484,14 @@
         place_kernel,
         grid=(ACQ_LOC // PLACE,),
         out_shape=jax.ShapeDtypeStruct((ACQ_LOC, 960, 128), f32),
-        in_specs=[pl.BlockSpec((8, 64, 16, 256), lambda m: (0, 0, 0, 0))],
+        in_specs=[pl.BlockSpec(memory_space=pl.ANY)],
         out_specs=pl.BlockSpec((PLACE, 960, 128), lambda m: (m, 0, 0)),
-        scratch_shapes=[pltpu.VMEM((2, 512 * 16, 128), f32), pltpu.VMEM((128, 512), f32)],
+        scratch_shapes=[
+            pltpu.VMEM((2, 512 * 16, 128), f32),
+            pltpu.VMEM((128, 512), f32),
+            pltpu.VMEM((8, 64, 16, 256), bf16),
+            dma((8,)),
+        ],
         compiler_params=params(),
         name="place",
     )(received)

time: 134 us -> 133 us (level)
  no operation moved by 1% of the time
where the time goes in v6:
time: 133 us; the launch traced here: 132 us
  Pallas kernels  132 us (99%)
    pallas_call x1, Pallas kernels, per_device(): pl.pallas_call(stack_kernel, out_shape=jax.ShapeDtypeStruct((N_GROUP, 8,...  123 us
    pallas_call x1, Pallas kernels, per_device(): pl.pallas_call(place_kernel, grid=(ACQ_LOC // PLACE,), out_shape=jax.Shap...  9.29 us

profile of v6, /device:TPU:1, one launch (start us, length us, event | category | flops | bytes accessed | tf_op | source)
XLA Modules:
  0.0 132.3 jit_solution(8825661794684876707)
XLA Ops:
  0.0 122.9 %stack.1 = bf16[8,8,8,16,256]{4,3,2,1,0:T(8,128)(2,1)} custom-call(f32[16,960,128]{2,1,0:T(8,128)} %bitcast.19, s32[8,16]{1,0:T(8,128)} %bitcast.20, s32[8,16]{1,0:T(8,128)} %bitcast.21, f32[1,15]{1,0:T(1,128)} %bitcast.22, s32[8]{0:T(128)} %row_radius_ref.1, s32[64]{0:T(128)} %col_radius_ref.1), custom_call_target="tpu_custom_call" | custom-call | tf_op jit(solution)/shard_map/stack/pallas_call | solution.py:439
  123.0 9.3 %place.1 = f32[15,960,128]{2,1,0:T(8,128)} custom-call(bf16[8,64,16,256]{3,2,1,0:T(8,128)(2,1)} %bitcast.18), custom_call_target="tpu_custom_call" | custom-call | tf_op jit(solution)/shard_map/place/pallas_call | solution.py:483
